TPU v7x, 256 devices: a whole 4x4x8 slice. The times are simulated.
256 devices in a mesh: dp: 4 (over z_lo), din: 8 (over y, core), dout: 8 (over z_hi, x).
Axes of the slice: x: 4, y: 4, z: 8 (z_hi: 2, z_lo: 4; z = z_hi * 4 + z_lo), core: 2. Of those that a mesh axis runs over, the one named last changes fastest.
Arguments:
- tokens: bfloat16 [1024, 8192], P(('dp', 'dout'), 'din'), may hold values from -6 to 6
- out_grad: bfloat16 [1024, 8192], P(('dp', 'dout'), 'din'), may hold values from -6 to 6
- gate_weight: bfloat16 [8192, 15360], P('din', 'dout'), may hold values from -0.0625 to 0.0625
- up_weight: bfloat16 [8192, 15360], P('din', 'dout'), may hold values from -0.0625 to 0.0625
- down_weight: bfloat16 [15360, 8192], P('dout', 'din'), may hold values from -0.046875 to 0.046875
- gate_step: float32 [15360], P('dout'), may hold values from 0.0027621358 to 0.011048543
- up_step: float32 [15360], P('dout'), may hold values from 0.0027621358 to 0.011048543
- down_step: float32 [8192], P('din'), may hold values from 0.0020171788 to 0.008068715
- outlier_in: int32 [128], P('din'), may hold values from 0 to 8191, as said below
- outlier_hidden: int32 [128], P('dout'), may hold values from 0 to 15359, as said below
Outputs:
- d_tokens: bfloat16 [1024, 8192], P(('dp', 'dout'), 'din')
- gate_step_grad: float32 [15360], P('dout')
- up_step_grad: float32 [15360], P('dout')
- down_step_grad: float32 [8192], P('din')
Inputs may be any that keep to these rules, and one draw needn't show every extreme that they name: `outlier_in`: sorted ascending and distinct; exactly 16 of them in each aligned block of 1024 channels. `outlier_hidden`: sorted ascending and distinct; exactly 16 of them in each aligned block of 1920 hidden units.
All inputs are finite; a program needn't handle non-finite values.
Results may differ from a plain program's by a relative error of at most 0.0072.
Values may be sent and summed in bfloat16 or wider, within the bound.
A program may use at most 128 MiB of HBM per device.

v0:
```python
import math

import jax
import jax.numpy as jnp
from jax import lax
from jax.sharding import PartitionSpec as P

D = 8192
FF = 15360
TOK_DEV = 256


QUANT_TOP = 7.0
SOFT_ROUND = 0.9
FULL_TURN = 2.0 * math.pi


def soft_quant(weight, step_size, keep_rows):
    ratio = weight.astype(jnp.float32) / step_size[None, :]
    squash = jnp.tanh(ratio / QUANT_TOP)
    level_value = QUANT_TOP * squash
    phase_angle = FULL_TURN * level_value
    shaped = level_value - SOFT_ROUND * jnp.sin(phase_angle) / FULL_TURN
    slope_value = (1.0 - SOFT_ROUND * jnp.cos(phase_angle)) * (1.0 - squash * squash)
    quantized = jnp.where(
        keep_rows[:, None], weight.astype(jnp.float32), step_size[None, :] * shaped
    ).astype(jnp.bfloat16)
    factor = jnp.where(keep_rows[:, None], jnp.float32(0.0), shaped - ratio * slope_value).astype(
        jnp.bfloat16
    )
    return (quantized, factor)


def swiglu_back(summed, hid_cols):
    gate_pre = summed[:, :hid_cols]
    up_pre = summed[:, hid_cols : 2 * hid_cols]
    back_grad = summed[:, 2 * hid_cols :]
    logistic = jax.nn.sigmoid(gate_pre)
    d_gate = back_grad * up_pre * logistic * (1.0 + gate_pre * (1.0 - logistic))
    d_up = back_grad * gate_pre * logistic
    hidden = gate_pre * logistic * up_pre
    return jnp.concatenate([d_gate, d_up, hidden], axis=1).astype(jnp.bfloat16)


def shards(
    tokens,
    out_grad,
    gate_weight,
    up_weight,
    down_weight,
    gate_step,
    up_step,
    down_step,
    outlier_in,
    outlier_hidden,
):
    in_rows = gate_weight.shape[0]
    hid_cols = gate_weight.shape[1]
    in_start = lax.axis_index("din") * in_rows
    hid_start = lax.axis_index("dout") * hid_cols
    keep_in = jnp.any(
        (jnp.arange(in_rows, dtype=jnp.int32) + in_start)[:, None] == outlier_in[None, :], axis=1
    )
    keep_hidden = jnp.any(
        (jnp.arange(hid_cols, dtype=jnp.int32) + hid_start)[:, None] == outlier_hidden[None, :],
        axis=1,
    )
    q_gate, f_gate = soft_quant(gate_weight, gate_step, keep_in)
    q_up, f_up = soft_quant(up_weight, up_step, keep_in)
    q_down, f_down = soft_quant(down_weight, down_step, keep_hidden)
    q_both = jnp.concatenate([q_gate, q_up], axis=1)
    f_both = jnp.concatenate([f_gate, f_up], axis=1)
    rows_all, grads_all = (
        lax.all_gather(tokens, "dout", axis=0, tiled=True),
        lax.all_gather(out_grad, "dout", axis=0, tiled=True),
    )
    forward = jnp.dot(rows_all, q_both, preferred_element_type=jnp.float32)
    backward = lax.dot_general(
        grads_all, q_down, (((1,), (1,)), ((), ())), preferred_element_type=jnp.float32
    )
    token_share = lax.psum_scatter(
        jnp.concatenate([forward, backward], axis=1), "din", scatter_dimension=0, tiled=True
    )
    packed = lax.all_gather(swiglu_back(token_share, hid_cols), "din", axis=0, tiled=True)
    d_both = packed[:, : 2 * hid_cols]
    hidden = packed[:, 2 * hid_cols :]
    d_tokens = lax.psum_scatter(
        lax.dot_general(
            d_both, q_both, (((1,), (1,)), ((), ())), preferred_element_type=jnp.float32
        ),
        "dout",
        scatter_dimension=0,
        tiled=True,
    ).astype(jnp.bfloat16)
    gate_terms = jnp.sum(
        d_both.astype(jnp.float32) * jnp.dot(rows_all, f_both, preferred_element_type=jnp.float32),
        axis=0,
    )
    down_terms = jnp.sum(
        grads_all.astype(jnp.float32) * jnp.dot(hidden, f_down, preferred_element_type=jnp.float32),
        axis=0,
    )
    gate_sums = lax.psum(gate_terms, ("dp", "din"))
    down_sums = lax.psum(down_terms, ("dp", "dout"))
    scale_in = 1.0 / math.sqrt(D * TOK_DEV)
    scale_hidden = 1.0 / math.sqrt(FF * TOK_DEV)
    return (
        d_tokens,
        gate_sums[:hid_cols] * scale_in,
        gate_sums[hid_cols:] * scale_in,
        down_sums * scale_hidden,
    )


def solution(mesh):
    return jax.shard_map(
        shards,
        mesh=mesh,
        in_specs=(
            P(("dp", "dout"), "din"),
            P(("dp", "dout"), "din"),
            P("din", "dout"),
            P("din", "dout"),
            P("dout", "din"),
            P("dout"),
            P("dout"),
            P("din"),
            P("din"),
            P("dout"),
        ),
        out_specs=(P(("dp", "dout"), "din"), P("dout"), P("dout"), P("din")),
        check_vma=False,
    )
```

profile of v0, /device:TPU:1, one launch (start us, length us, event | category | flops | bytes accessed | tf_op | source)
XLA Modules:
  0.0 565.7 jit_solution(6309760677355578901)
XLA Ops:
  7.2 0.0 reduce-scatter.7.cloned.1.call-start
  7.2 42.0 %all_gather.9 = bf16[256,1024]{1,0:T(8,128)(2,1)S(1)} all-gather(bf16[32,1024]{1,0:T(8,128)(2,1)} %param.10), channel_id=1, replica_groups=mesh['dp'=4,'din'=8,'dout'=8] {'dout'}, dimensions={0}, use_global_device_ids=true | all-gather | bytes 589824 | tf_op jit(solution)/shard_map/all_gather | solution.py:74
  49.2 39.4 %all_gather.10 = bf16[256,1024]{1,0:T(8,128)(2,1)S(1)} all-gather(bf16[32,1024]{1,0:T(8,128)(2,1)} %param.11), channel_id=1, replica_groups=mesh['dp'=4,'din'=8,'dout'=8] {'dout'}, dimensions={0}, use_global_device_ids=true | all-gather | bytes 589824 | tf_op jit(solution)/shard_map/all_gather | solution.py:75
  88.6 0.7 compare_reduce_fusion.1
  89.3 0.8 compare_reduce_fusion
  90.1 69.3 %select_convert_fusion.2 = (bf16[1024,1920]{1,0:T(8,128)(2,1)}, bf16[1024,1920]{1,0:T(8,128)(2,1)S(1)}, bf16[1024,1920]{1,0:T(8,128)(2,1)S(1)}, bf16[1024,1920]{1,0:T(8,128)(2,1)}) fusion(bf16[1024,1920]{1,0:T(8,128)(2,1)} %param.12, f32[1920]{0:T(1024)} %param.15, pred[1024]{0:T(1024)(128)(4,1)S(1)} %compare_reduce_fusion.1, f32[1920]{0:T(1024)} %param.16, ...), kind=kLoop, calls=%fused_computation.16 | loop fusion | flops 74711040 | bytes 23609344 | tf_op jit(solution)/shard_map/convert_element_type | solution.py:28
  159.4 0.0 copy-start
  159.4 0.0 copy-start.1
  159.4 0.0 copy-start.2
  159.4 0.0 copy-start.3
  159.4 2.4 convolution_bitcast_fusion
  161.8 0.0 copy-done
  161.8 1.6 copy-done.1
  163.3 1.0 copy-done.2
  164.3 0.0 copy-done.3
  164.3 30.4 %fusion.21 = f32[256,1920]{0,1:T(8,128)S(1)} fusion(bf16[256,1024]{1,0:T(8,128)(2,1)S(1)} %all_gather.10, bf16[1920,1024]{1,0:T(8,128)(2,1)S(1)} %copy-done.2, f32[1024]{0:T(1024)S(1)} %copy-done.3, pred[1920]{0:T(1024)(128)(4,1)S(1)} %compare_reduce_fusion), kind=kOutput, calls=%fused_computation.34 | convolution fusion | flops 1026293760 | bytes 6428544 | tf_op jit(solution)/shard_map/dot_general | solution.py:78
  194.7 3.0 pad_maximum_fusion.1
  197.7 6.5 %copy.24 = f32[256,5760]{1,0:T(8,128)} copy(f32[256,5760]{0,1:T(8,128)} %pad_maximum_fusion.1) | data formatting | bytes 11796480
  204.1 0.0 reduce-scatter.7.cloned.1.call-update
  204.1 0.0 all-gather.2.cloned.1.call-start
  204.2 55.1 %reduce-scatter.7.cloned.1.call-done = f32[32,5760]{1,0:T(8,128)} async-done(((f32[256,5760]{1,0:T(8,128)}), f32[32,5760]{1,0:T(8,128)}) %reduce-scatter.7.cloned.1.call-update) | async-done | bytes 737296 | tf_op jit(solution)/shard_map/reduce_scatter | solution.py:81
  259.2 1.3 multiply_convert_fusion.2
  260.6 0.8 pad_maximum_fusion.4
  261.3 0.0 all-gather.2.cloned.1.call-update
  261.4 0.0 reduce-scatter.5.cloned.1.call-start
  261.4 31.1 %all-gather.2.cloned.1.call-done = bf16[256,5760]{1,0:T(8,128)(2,1)} async-done(((bf16[32,5760]{1,0:T(8,128)(2,1)}), bf16[256,5760]{1,0:T(8,128)(2,1)}) %all-gather.2.cloned.1.call-update) | async-done | bytes 2949136 | tf_op jit(solution)/shard_map/all_gather | solution.py:84
  292.5 7.0 %fusion.16 = f32[256,1024]{1,0:T(8,128)} fusion(bf16[1024,1920]{1,0:T(8,128)(2,1)} %copy-done.1, bf16[1024,1920]{1,0:T(8,128)(2,1)} %copy-done, bf16[256,5760]{1,0:T(8,128)(2,1)} %all-gather.2.cloned.1.call-done), kind=kOutput, calls=%fused_computation.30 | convolution fusion | flops 2028994560 | bytes 10878976 | tf_op jit(solution)/shard_map/dot_general | solution.py:88
  299.6 0.0 reduce-scatter.5.cloned.1.call-update
  299.6 34.7 %fusion.29 = f32[1024]{0:T(1024)S(1)} fusion(bf16[1920,1024]{1,0:T(8,128)(2,1)} %param.14, f32[1024]{0:T(1024)S(1)} %copy-done.3, pred[1920]{0:T(1024)(128)(4,1)S(1)} %compare_reduce_fusion, bf16[256,1024]{1,0:T(8,128)(2,1)S(1)} %all_gather.10, bf16[256,5760]{1,0:T(8,128)(2,1)} %all-gather.2.cloned.1.call-done), kind=kOutput, calls=%fused_computation.38 | convolution fusion | flops 1038875648 | bytes 5449600 | tf_op jit(solution)/shard_map/dot_general | solution.py:100
  334.3 74.1 %psum.15 = f32[1024]{0:T(1024)S(1)} all-reduce(f32[1024]{0:T(1024)S(1)} %fusion.29), channel_id=1, replica_groups=mesh['dp'=4,'din'=8,'dout'=8] {'dp','dout'}, use_global_device_ids=true, to_apply=%region_7.8 | all-reduce | flops 1024 | bytes 8192 | tf_op jit(solution)/shard_map/psum | solution.py:104
  408.4 6.2 %fusion.25 = f32[3840]{0:T(1024)S(1)} fusion(bf16[256,1024]{1,0:T(8,128)(2,1)S(1)} %all_gather.9, bf16[1024,1920]{1,0:T(8,128)(2,1)} %get-tuple-element.14, bf16[1024,1920]{1,0:T(8,128)(2,1)} %get-tuple-element.4, bf16[256,5760]{1,0:T(8,128)(2,1)} %all-gather.2.cloned.1.call-done), kind=kOutput, calls=%fused_computation.36 | convolution fusion | flops 2031939840 | bytes 10370048 | tf_op jit(solution)/shard_map/dot_general | solution.py:96
  414.6 141.9 %psum.14 = f32[3840]{0:T(1024)S(1)} all-reduce(f32[3840]{0:T(1024)S(1)} %fusion.25), channel_id=1, replica_groups=mesh['dp'=4,'din'=8,'dout'=8] {'dp','din'}, use_global_device_ids=true, to_apply=%region_5.6 | all-reduce | flops 3840 | bytes 30720 | tf_op jit(solution)/shard_map/psum | solution.py:103
  556.4 0.6 broadcast_multiply_fusion
  557.0 0.6 slice_multiply_fusion
  557.6 0.0 reduce-scatter.5.cloned.1.call-done
  557.6 1.5 convert_element_type.46
  (2 shorter events, 0.0 us)
Async XLA Ops:
  7.2 252.1 %reduce-scatter.7.cloned.1.call-start = ((), (), s32[]{:S(2)}) async-start(), calls=%async_computation.4 | async-start | bytes 6635520 | tf_op jit(solution)/shard_map/reduce_scatter | solution.py:81
  159.4 2.4 copy-start
  159.4 4.0 copy-start.1
  159.4 5.0 copy-start.2
  159.4 4.9 copy-start.3
  204.1 88.4 %all-gather.2.cloned.1.call-start = ((), (), s32[]{:S(2)}) async-start(), calls=%async_computation.2 | async-start | bytes 3317760 | tf_op jit(solution)/shard_map/all_gather | solution.py:84
  261.4 296.3 %reduce-scatter.5.cloned.1.call-start = ((), (), s32[]{:S(2)}) async-start(), calls=%async_computation.3 | async-start | bytes 1179648 | tf_op jit(solution)/shard_map/reduce_scatter | solution.py:87
Sparse Core Ops, SparseCore 0:
  204.2 54.9 reduce-scatter.6
  261.5 31.0 all-gather.1
  299.7 84.9 reduce-scatter.4
where the time goes:
time: 574 us; the launch traced here: 566 us
  blocking collectives  297 us (52%)
  waiting for transfers between devices  86.2 us (15%)
  matrix products  80.6 us (14%)
  other arithmetic  78.6 us (14%)
  between operations  13.8 us (2%)
  local copies, waits for them, and re-layouts  9.02 us (2%)
    psum x1, blocking collectives, shards(): gate_sums = lax.psum(gate_terms, ('dp', 'din'))  142 us
    psum x1, blocking collectives, shards(): down_sums = lax.psum(down_terms, ('dp', 'dout'))  74.1 us
    convert_element_type x1, other arithmetic, soft_quant(): jnp.where(keep_rows[:, None], jnp.float32(0.0), shaped - ratio * slope_va...  69.3 us
    reduce_scatter x1, waiting for transfers between devices, shards(): lax.psum_scatter(jnp.concatenate([forward, backward], axis=1), 'din', sca...  55.1 us
    all_gather x1, blocking collectives, shards(): lax.all_gather(tokens, 'dout', axis=0, tiled=True)  42 us
    all_gather x1, blocking collectives, shards(): lax.all_gather(out_grad, 'dout', axis=0, tiled=True)  39.4 us
    dot_general x1, matrix products, shards(): jnp.dot(hidden, f_down, preferred_element_type=jnp.float32)  34.7 us
    all_gather x1, waiting for transfers between devices, shards(): lax.all_gather(swiglu_back(token_share, hid_cols), 'din', axis=0, tiled=T...  31.1 us
  transfers between devices with their start and end apart: 3, of which 2 were waited for; matrix products, arithmetic and copies ran while one was open for 7% of the time, Pallas kernels for 0%

commit v1 on v0

v1 whole, which is shorter than its diff:
```python
import math

import jax
import jax.numpy as jnp
from jax import lax
from jax.experimental import pallas as pl
from jax.experimental.pallas import tpu as pltpu
from jax.sharding import PartitionSpec as P

D = 8192
FF = 15360
TOK_DEV = 256
SCALE_IN = 1.0 / math.sqrt(D * TOK_DEV)
SCALE_HID = 1.0 / math.sqrt(FF * TOK_DEV)

KB = 1024
HB = 1920
N = 5
C = HB // N
C2, C3 = 2 * C, 3 * C
T = 256
HALF = T // 2
BLK = 32

MESH = pl.DeviceIdType.MESH
BF, F32 = jnp.bfloat16, jnp.float32

SIN = (3.14158202, -5.16714276, 2.5418987, -0.55463534)


def quant(w, step, inv7, keep):
    w = w.astype(F32)
    x = w * inv7
    t = jnp.tanh(x)
    c = 7.0 * t
    r = c - jnp.round(c)
    u = r * r
    p = jnp.float32(SIN[3])
    for k in (2, 1, 0):
        p = p * u + jnp.float32(SIN[k])
    sn = p * r
    s2 = sn * sn
    d = jnp.maximum(1.0 - s2, 1e-12)
    cs = d * lax.rsqrt(d)
    shaped = c - sn * cs * jnp.float32(0.9 / math.pi)
    slope7 = (0.7 + 12.6 * s2) * (1.0 - t * t)
    q = jnp.where(keep, w, step * shaped)
    f = jnp.where(keep, 0.0, shaped - x * slope7)
    return q.astype(BF), f.astype(BF)


def remote(src, dst, ssem, rsem, dev):
    return pltpu.make_async_remote_copy(
        src_ref=src, dst_ref=dst, send_sem=ssem, recv_sem=rsem, device_id=dev, device_id_type=MESH
    )


def dot(a, b):
    return jnp.dot(a, b, preferred_element_type=F32)


def dot_t(a, b):
    return lax.dot_general(a, b, (((1,), (1,)), ((), ())), preferred_element_type=F32)


def kernel(
    tok_hbm, og_hbm, gw, uw, dw, gs, us, ds, oi, oh,
    dt_out, gg_out, ug_out, dg_out,
    tg, wgu, fgu, wd, fd, kin, khid, sgu, igu, idn,
    pre, send1, recv1, send2, recv2, act,
    acc, esend, erecv, gt, gslot, gdp, dterm, dslot, dz,
    lsem, gusem, dsem, zs, zr, xs, xr, s1s, s1r, y2s, y2r, ags, agr, s2s, s2r,
    es, er, gs_s, gs_r, gp_s, gp_r, ds_s, ds_r, dz_s, dz_r,
):
    dp = lax.axis_index("dp")
    din = lax.axis_index("din")
    dout = lax.axis_index("dout")
    y, c = din // 2, din % 2
    zh, x = dout // 4, dout % 4

    def at_y(k, core):
        return (dp, (k % 4) * 2 + core, dout)

    def at_x(k, hi):
        return (dp, din, hi * 4 + k % 4)

    sibling = (dp, y * 2 + (1 - c), dout)

    def rows_of(block):
        return pl.ds(pl.multiple_of((block * BLK + c * HALF) % T, BLK), BLK)

    mine = rows_of(dout)
    own = [
        pltpu.make_async_copy(tok_hbm, tg.at[0, mine], lsem.at[0]),
        pltpu.make_async_copy(og_hbm, tg.at[1, mine], lsem.at[1]),
    ]
    for cp in own:
        cp.start()

    def weight_copies(i):
        cols = pl.ds(pl.multiple_of(i * C, 128), C)
        return [
            pltpu.make_async_copy(gw.at[:, cols], wgu.at[i, :, pl.ds(0, C)], gusem.at[i, 0]),
            pltpu.make_async_copy(uw.at[:, cols], wgu.at[i, :, pl.ds(C, C)], gusem.at[i, 1]),
            pltpu.make_async_copy(dw.at[cols], wd.at[i], dsem.at[i]),
        ]

    @pl.loop(0, N)
    def _(i):
        for cp in weight_copies(i):
            cp.start()

    barrier = pltpu.get_barrier_semaphore()

    def greet(dev):
        pl.semaphore_signal(barrier, inc=1, device_id=dev, device_id_type=MESH)

    for k in range(1, 8):
        greet((dp, (din + k) % 8, dout))
        greet((dp, din, (dout + k) % 8))
    for k in range(1, 4):
        greet(((dp + k) % 4, din, dout))
        greet(((dp + k) % 4, din, (dout + 4) % 8))

    def fill_mask(ref, values, start, rows):
        @pl.loop(0, rows // 64)
        def _(b):
            idx = lax.broadcasted_iota(jnp.int32, (64, 128), 0) + (b * 64 + start)
            hit = idx == values[0]
            for k in range(1, 16):
                hit = hit | (idx == values[k])
            ref[pl.ds(pl.multiple_of(b * 64, 64), 64), :] = jnp.where(hit, 1.0, 0.0)

    fill_mask(kin, oi, din * KB, KB)
    fill_mask(khid, oh, dout * HB, HB)
    for i in range(N):
        sgu[i, :, 0:C] = gs[:, i * C : (i + 1) * C]
        sgu[i, :, C:C2] = us[:, i * C : (i + 1) * C]
    igu[...] = 1.0 / (7.0 * sgu[...])
    idn[...] = 1.0 / (7.0 * ds[...])
    acc[...] = jnp.zeros_like(acc)
    dterm[...] = jnp.zeros_like(dterm)

    pl.semaphore_wait(barrier, 20)
    for cp in own:
        cp.wait()

    zcopy = remote(tg.at[:, mine], tg.at[:, mine], zs, zr, at_x(x, 1 - zh))
    zcopy.start()
    theirs = rows_of((dout + 4) % 8)

    def xcopy(which, k):
        rows = mine if which == 0 else theirs
        return remote(tg.at[:, rows], tg.at[:, rows], xs.at[which, k - 1], xr.at[which, k - 1], at_x(x + k, zh))

    def xarrive(which, k):
        rows = rows_of((x + 4 - k) % 4 + 4 * (zh if which == 0 else 1 - zh))
        return remote(tg.at[:, rows], tg.at[:, rows], xs.at[which, k - 1], xr.at[which, k - 1], at_x(x + k, zh))

    for k in (1, 3, 2):
        xcopy(0, k).start()

    def do_quant(i):
        for cp in weight_copies(i):
            cp.wait()
        for part in range(2):
            lanes = pl.ds(part * C, C)
            step, inv = sgu[i, :, lanes], igu[i, :, lanes]

            def body(b, carry):
                rows = pl.ds(pl.multiple_of(b * 64, 64), 64)
                keep = kin[rows, :][:, :1] > 0
                q, f = quant(wgu[i, rows, lanes], step, inv, keep)
                wgu[i, rows, lanes] = q
                fgu[i, rows, lanes] = f
                return carry

            lax.fori_loop(0, KB // 64, body, 0, unroll=2)
        for part in range(2):
            lanes = pl.ds(part * 512, 512)
            step, inv = ds[:, lanes], idn[:, lanes]

            def body(b, carry):
                rows = pl.ds(pl.multiple_of(b * 64, 64), 64)
                keep = khid[pl.ds(pl.multiple_of(i * C + b * 64, 64), 64), :][:, :1] > 0
                q, f = quant(wd[i, rows, lanes], step, inv, keep)
                wd[i, rows, lanes] = q
                fd[i, rows, lanes] = f
                return carry

            lax.fori_loop(0, C // 64, body, 0, unroll=2)

    def sib1(i):
        return remote(send1.at[i], recv1.at[i], s1s.at[i], s1r.at[i], sibling)

    def do_forward(i):
        for n in range(3):
            cols = slice(n * 256, (n + 1) * 256)
            z = dot(tg[0], wgu[i, :, cols])
            pre[i, :, cols] = z[:HALF]
            send1[i, :, cols] = z[HALF:].astype(BF)
        z = dot_t(tg[1], wd[i])
        pre[i, :, C2:] = z[:HALF]
        send1[i, :, C2:] = z[HALF:].astype(BF)
        sib1(i).start()

    def ycopy(i, k):
        rows = pl.ds(pl.multiple_of(((y + k) % 4) * BLK, BLK), BLK)
        return remote(send2.at[i, rows], recv2.at[i, k - 1], y2s.at[i, k - 1], y2r.at[i, k - 1], at_y(y + k, c))

    def do_pair_sum(i):
        sib1(i).wait_recv()
        total = pre[i] + recv1[i].astype(F32)
        pre[i] = total
        send2[i] = total.astype(BF)
        for k in (2, 1, 3):
            ycopy(i, k).start()

    myrow = pl.ds(pl.multiple_of(y * BLK, BLK), BLK)

    def agcopy(i, k):
        return remote(act.at[i, myrow], act.at[i, myrow], ags.at[i, k - 1], agr.at[i, k - 1], at_y(y + k, c))

    def agarrive(i, k):
        rows = pl.ds(pl.multiple_of(((y + 4 - k) % 4) * BLK, BLK), BLK)
        return remote(act.at[i, rows], act.at[i, rows], ags.at[i, k - 1], agr.at[i, k - 1], at_y(y + k, c))

    def do_act(i):
        for k in (1, 3, 2):
            ycopy(i, k).wait_recv()
        own_rows = pre[i, myrow]

        def summed(lo, hi):
            v = own_rows[:, lo:hi]
            for k in range(3):
                v = v + recv2[i, k, :, lo:hi].astype(F32)
            return v

        gate, up, back = summed(0, C), summed(C, C2), summed(C2, C3)
        p = jax.nn.sigmoid(gate)
        gp = gate * p
        act[i, myrow, 0:C] = (back * up * p * (1.0 + gate * (1.0 - p))).astype(BF)
        act[i, myrow, C:C2] = (back * gp).astype(BF)
        act[i, myrow, C2:C3] = (gp * up).astype(BF)
        for k in (2, 1, 3):
            agcopy(i, k).start()

    def sib2(i):
        return remote(
            act.at[i, pl.ds(0, HALF)], act.at[i, pl.ds(HALF, HALF)], s2s.at[i], s2r.at[i], sibling
        )

    def do_share(i):
        for k in (1, 3, 2):
            agarrive(i, k).wait_recv()
        sib2(i).start()

    def do_back(i):
        sib2(i).wait_recv()
        for n in range(4):
            cols = slice(n * 256, (n + 1) * 256)
            acc[:, cols] += dot_t(act[i, :, 0:C2], wgu[i, cols, :])
        for n in range(3):
            cols = slice(n * 256, (n + 1) * 256)
            z = dot(tg[0], fgu[i, :, cols])
            term = jnp.sum(act[i, :, cols].astype(F32) * z, axis=0, keepdims=True)
            gt[i, :, cols] = term
        for n in range(4):
            cols = slice(n * 256, (n + 1) * 256)
            z = dot(act[i, :, C2:C3], fd[i, :, cols])
            dterm[:, cols] += jnp.sum(tg[1, :, cols].astype(F32) * z, axis=0, keepdims=True)

    @pl.loop(0, N + 3)
    def _(i):
        @pl.when(i < N)
        def _():
            do_quant(i)

        @pl.when(i == 0)
        def _():
            zcopy.wait_recv()
            for k in (1, 3, 2):
                xcopy(1, k).start()

        @pl.when(i >= 3)
        def _():
            do_share(i - 3)

        @pl.when(i == 1)
        def _():
            for which in range(2):
                for k in range(1, 4):
                    xarrive(which, k).wait_recv()

        @pl.when((i >= 1) & (i < N + 1))
        def _():
            do_forward(i - 1)

        @pl.when((i >= 2) & (i < N + 2))
        def _():
            do_act(i - 2)

        @pl.when((i >= 1) & (i < N + 1))
        def _():
            do_pair_sum(i - 1)

        @pl.when(i >= 3)
        def _():
            do_back(i - 3)

    esend[...] = acc[...].astype(BF)

    def ecopy(k):
        return remote(
            esend.at[rows_of((dout + k) % 8)], erecv.at[k - 1], es.at[k - 1], er.at[k - 1],
            (dp, din, (dout + k) % 8),
        )

    for k in (4, 3, 5, 2, 6, 1, 7):
        ecopy(k).start()

    gslot[din] = gt[...]
    dslot[x] = dterm[...]

    def gcopy(k):
        return remote(gt, gslot.at[din], gs_s.at[k - 1], gs_r.at[din], (dp, (din + k) % 8, dout))

    def garrive(k):
        src = (din + k) % 8
        return remote(gt, gslot.at[src], gs_s.at[k - 1], gs_r.at[src], (dp, src, dout))

    def dcopy(k):
        return remote(dterm, dslot.at[x], ds_s.at[k - 1], ds_r.at[x], at_x(x + k, zh))

    def darrive(k):
        src = (x + k) % 4
        return remote(dterm, dslot.at[src], ds_s.at[k - 1], ds_r.at[src], at_x(src, zh))

    for k in range(1, 4):
        dcopy(k).start()
    for k in range(1, 8):
        gcopy(k).start()
    for k in range(1, 4):
        darrive(k).wait_recv()
    part = dslot[0]
    for k in range(1, 4):
        part = part + dslot[k]
    zi = zh * 4 + dp
    dz[zi] = part

    def at_z(k):
        return (k % 4, din, (k // 4) * 4 + x)

    def zzcopy(k):
        return remote(dz.at[zi], dz.at[zi], dz_s.at[k - 1], dz_r.at[zi], at_z((zi + k) % 8))

    def zzarrive(k):
        src = (zi + k) % 8
        return remote(dz.at[src], dz.at[src], dz_s.at[k - 1], dz_r.at[src], at_z(src))

    for k in range(1, 8):
        zzcopy(k).start()
    for k in range(1, 8):
        garrive(k).wait_recv()
    part = gslot[0]
    for k in range(1, 8):
        part = part + gslot[k]
    gdp[dp] = part

    def gpcopy(k):
        return remote(gdp.at[dp], gdp.at[dp], gp_s.at[k - 1], gp_r.at[dp], ((dp + k) % 4, din, dout))

    def gparrive(k):
        src = (dp + k) % 4
        return remote(gdp.at[src], gdp.at[src], gp_s.at[k - 1], gp_r.at[src], (src, din, dout))

    for k in range(1, 4):
        gpcopy(k).start()
    for k in range(1, 8):
        ecopy(k).wait_recv()
    total = acc[rows_of(dout), :]
    for k in range(7):
        total = total + erecv[k].astype(F32)
    dt_out[...] = total.astype(BF)
    for k in range(1, 4):
        gparrive(k).wait_recv()
    part = gdp[0]
    for k in range(1, 4):
        part = part + gdp[k]
    part = part * SCALE_IN
    for i in range(N):
        gg_out[:, i * C : (i + 1) * C] = part[i, :, 0:C]
        ug_out[:, i * C : (i + 1) * C] = part[i, :, C:C2]
    for k in range(1, 8):
        zzarrive(k).wait_recv()
    part = dz[0]
    for k in range(1, 8):
        part = part + dz[k]
    dg_out[...] = part * SCALE_HID

    zcopy.wait_send()
    for k in range(1, 4):
        for which in range(2):
            xcopy(which, k).wait_send()
        dcopy(k).wait_send()
        gpcopy(k).wait_send()
    for k in range(1, 8):
        ecopy(k).wait_send()
        gcopy(k).wait_send()
        zzcopy(k).wait_send()

    @pl.loop(0, N)
    def _(i):
        sib1(i).wait_send()
        sib2(i).wait_send()
        for k in range(1, 4):
            ycopy(i, k).wait_send()
            agcopy(i, k).wait_send()


def shards(tokens, out_grad, gate_weight, up_weight, down_weight, gate_step, up_step, down_step, outlier_in, outlier_hidden):
    hbm = pl.BlockSpec(memory_space=pl.ANY)
    vmem = pl.BlockSpec(memory_space=pltpu.VMEM)
    smem = pl.BlockSpec(memory_space=pltpu.SMEM)
    V, S = pltpu.VMEM, pltpu.SemaphoreType.DMA
    d_tokens, gg, ug, dg = pl.pallas_call(
        kernel,
        out_shape=(
            jax.ShapeDtypeStruct((BLK, KB), BF),
            jax.ShapeDtypeStruct((1, HB), F32),
            jax.ShapeDtypeStruct((1, HB), F32),
            jax.ShapeDtypeStruct((1, KB), F32),
        ),
        in_specs=[hbm, hbm, hbm, hbm, hbm, vmem, vmem, vmem, smem, smem],
        out_specs=(vmem, vmem, vmem, vmem),
        scratch_shapes=[
            V((2, T, KB), BF),
            V((N, KB, C2), BF),
            V((N, KB, C2), BF),
            V((N, C, KB), BF),
            V((N, C, KB), BF),
            V((KB, 128), F32),
            V((HB, 128), F32),
            V((N, 1, C2), F32),
            V((N, 1, C2), F32),
            V((1, KB), F32),
            V((N, HALF, C3), F32),
            V((N, HALF, C3), BF),
            V((N, HALF, C3), BF),
            V((N, HALF, C3), BF),
            V((N, 3, BLK, C3), BF),
            V((N, T, C3), BF),
            V((T, KB), F32),
            V((T, KB), BF),
            V((7, BLK, KB), BF),
            V((N, 1, C2), F32),
            V((8, N, 1, C2), F32),
            V((4, N, 1, C2), F32),
            V((1, KB), F32),
            V((4, 1, KB), F32),
            V((8, 1, KB), F32),
            S((2,)),
            S((N, 2)),
            S((N,)),
            S, S,
            S((2, 3)), S((2, 3)),
            S((N,)), S((N,)),
            S((N, 3)), S((N, 3)),
            S((N, 3)), S((N, 3)),
            S((N,)), S((N,)),
            S((7,)), S((7,)),
            S((7,)), S((8,)),
            S((3,)), S((4,)),
            S((3,)), S((4,)),
            S((7,)), S((8,)),
        ],
        compiler_params=pltpu.CompilerParams(
            collective_id=0, has_side_effects=True, vmem_limit_bytes=56 * 2**20
        ),
        name="swiglu_back",
    )(
        tokens, out_grad, gate_weight, up_weight, down_weight,
        gate_step.reshape(1, HB), up_step.reshape(1, HB), down_step.reshape(1, KB),
        outlier_in, outlier_hidden,
    )
    return d_tokens, gg.reshape(HB), ug.reshape(HB), dg.reshape(KB)


def solution(mesh):
    return jax.shard_map(
        shards,
        mesh=mesh,
        in_specs=(
            P(("dp", "dout"), "din"),
            P(("dp", "dout"), "din"),
            P("din", "dout"),
            P("din", "dout"),
            P("dout", "din"),
            P("dout"),
            P("dout"),
            P("din"),
            P("din"),
            P("dout"),
        ),
        out_specs=(P(("dp", "dout"), "din"), P("dout"), P("dout"), P("din")),
        check_vma=False,
    )
```

time: 574 us -> 108 us (0.19); the launches traced: 566 us -> 106 us
  blocking collectives: 297 us -> 0 us
  Pallas kernels: 0 us -> 97.7 us
  waiting for transfers between devices: 86.2 us -> 0 us
  matrix products: 80.6 us -> 0 us
  other arithmetic: 78.6 us -> 2.63 us
  between operations: 13.8 us -> 0.64 us
    psum x2 -> x0, blocking collectives: 216 us -> none  [the longest x1 142 us: shards(): gate_sums = lax.psum(gate_terms, ('dp', 'din'))]
    pallas_call x0 -> x1, Pallas kernels: none -> 97.7 us  [shards(): pl.pallas_call(kernel, out_shape=(jax.ShapeDtypeStruct((BLK, KB), BF), ja...]
    all_gather x2 -> x0, blocking collectives: 81.3 us -> none  [the longest x1 42 us: shards(): lax.all_gather(tokens, 'dout', axis=0, tiled=True)]
    dot_general x5 -> x0, matrix products: 80.6 us -> none  [the longest x1 34.7 us: shards(): jnp.dot(hidden, f_down, preferred_element_type=jnp.float32)]
    convert_element_type x2 -> x0, other arithmetic: 70.8 us -> none  [the longest x1 69.3 us: soft_quant(): jnp.where(keep_rows[:, None], jnp.float32(0.0), shaped - ratio * slope_va...]
    reduce_scatter x2 -> x0, waiting for transfers between devices: 55.1 us -> none  [the longest x1 55.1 us: shards(): lax.psum_scatter(jnp.concatenate([forward, backward], axis=1), 'din', sca...]
    all_gather x1 -> x0, waiting for transfers between devices: 31.1 us -> none  [shards(): lax.all_gather(swiglu_back(token_share, hid_cols), 'din', axis=0, tiled=T...]
    unnamed x9 -> x2, local copies, waits for them, and re-layouts: 9.02 us -> 2.75 us
  transfers between devices with their start and end apart: 3 -> 0, of which waited for: 2 -> 0; matrix products, arithmetic and copies ran while one was open for 7% -> 0% of each run, Pallas kernels for 0% -> 0%
where the time goes in v1:
time: 108 us; the launch traced here: 106 us
  Pallas kernels  97.7 us (90%)
  local copies, waits for them, and re-layouts  5.34 us (5%)
  other arithmetic  2.63 us (2%)
    pallas_call x1, Pallas kernels, shards(): pl.pallas_call(kernel, out_shape=(jax.ShapeDtypeStruct((BLK, KB), BF), ja...  97.7 us
    unnamed x2, local copies, waits for them, and re-layouts  2.75 us
    pallas_call x2, other arithmetic, shards(): pl.pallas_call(kernel, out_shape=(jax.ShapeDtypeStruct((BLK, KB), BF), ja...  2.63 us

profile of v1, /device:TPU:1, one launch (start us, length us, event | category | flops | bytes accessed | tf_op | source)
XLA Modules:
  0.0 106.3 jit_solution(3639218133145060002)
XLA Ops:
  0.6 1.3 %reshape.26.gs = f32[1,1920]{1,0:T(1,128)} reshape(f32[1920]{0:T(1024)} %param.15) | data formatting | bytes 15360 | tf_op jit(solution)/shard_map/reshape | solution.py:483
  1.9 1.3 %reshape.27.us = f32[1,1920]{1,0:T(1,128)} reshape(f32[1920]{0:T(1024)} %param.16) | data formatting | bytes 15360 | tf_op jit(solution)/shard_map/reshape | solution.py:483
  3.2 97.7 %swiglu_back.1 = (bf16[32,1024]{1,0:T(8,128)(2,1)}, f32[1,1920]{1,0:T(1,128)}, f32[1,1920]{1,0:T(1,128)}, f32[1,1024]{1,0:T(1,128)}) custom-call(bf16[32,1024]{1,0:T(8,128)(2,1)} %tok_hbm.1, bf16[32,1024]{1,0:T(8,128)(2,1)} %og_hbm.1, bf16[1024,1920]{1,0:T(8,128)(2,1)} %gw.1, bf16[1024,1920]{1,0:T(8,128)(2,1)} %uw.1, bf16[1920,1024]{1,0:T(8,128)(2,1)} %dw.1, ...), custom_call_target="tpu_custom_call" | custom-call | tf_op jit(solution)/shard_map/swiglu_back/pallas_call | solution.py:426
  100.9 1.3 %reduce = f32[1920]{0:T(1024)} reduce(f32[1,1920]{1,0:T(1,128)} %get-tuple-element.9, f32[]{:T(128)} %constant), dimensions={0}, to_apply=%get-tuple-element.9.reduce_sub_computation | reduce | bytes 15364 | tf_op jit(solution)/shard_map/swiglu_back/pallas_call | solution.py:426
  102.2 1.3 %reduce.1 = f32[1920]{0:T(1024)} reduce(f32[1,1920]{1,0:T(1,128)} %get-tuple-element.10, f32[]{:T(128)} %constant), dimensions={0}, to_apply=%get-tuple-element.10.reduce_sub_computation | reduce | bytes 15364 | tf_op jit(solution)/shard_map/swiglu_back/pallas_call | solution.py:426
  103.5 1.5 %copy.16 = bf16[32,1024]{1,0:T(8,128)(2,1)} copy(bf16[32,1024]{1,0:T(8,128)(2,1)} %get-tuple-element.16) | data formatting | bytes 131072
  105.0 1.3 %copy.17 = f32[1024]{0:T(1024)} copy(f32[1024]{0:T(1024)} %bitcast.3) | data formatting | bytes 8192

commit v2 on v1

--- a/solution.py
+++ b/solution.py
@@ -65,12 +65,12 @@
 
 def kernel(
     tok_hbm, og_hbm, gw, uw, dw, gs, us, ds, oi, oh,
-    dt_out, gg_out, ug_out, dg_out,
-    tg, wgu, fgu, wd, fd, kin, khid, sgu, igu, idn,
+    dt_out, gu_out, dg_out,
+    tg, wgu, fgu, wd, fd, kin, khid, sgu, igu, sdn, idn,
     pre, send1, recv1, send2, recv2, act,
-    acc, esend, erecv, gt, gslot, gdp, dterm, dslot, dz,
+    acc, esend, erecv, ezsend, ezrecv, gt, gslot, gdp, dterm, dslot, dz,
     lsem, gusem, dsem, zs, zr, xs, xr, s1s, s1r, y2s, y2r, ags, agr, s2s, s2r,
-    es, er, gs_s, gs_r, gp_s, gp_r, ds_s, ds_r, dz_s, dz_r,
+    es, er, ezs, ezr, gs_s, gs_r, gp_s, gp_r, ds_s, ds_r, dz_s, dz_r,
 ):
     dp = lax.axis_index("dp")
     din = lax.axis_index("din")
@@ -102,13 +102,17 @@
         return [
             pltpu.make_async_copy(gw.at[:, cols], wgu.at[i, :, pl.ds(0, C)], gusem.at[i, 0]),
             pltpu.make_async_copy(uw.at[:, cols], wgu.at[i, :, pl.ds(C, C)], gusem.at[i, 1]),
-            pltpu.make_async_copy(dw.at[cols], wd.at[i], dsem.at[i]),
         ]
+
+    def down_copy(i):
+        rows = pl.ds(pl.multiple_of(i * C, 128), C)
+        return pltpu.make_async_copy(dw.at[rows], wd.at[i], dsem.at[i])
 
     @pl.loop(0, N)
     def _(i):
         for cp in weight_copies(i):
             cp.start()
+        down_copy(i).start()
 
     barrier = pltpu.get_barrier_semaphore()
 
@@ -134,10 +138,11 @@
     fill_mask(kin, oi, din * KB, KB)
     fill_mask(khid, oh, dout * HB, HB)
     for i in range(N):
-        sgu[i, :, 0:C] = gs[:, i * C : (i + 1) * C]
-        sgu[i, :, C:C2] = us[:, i * C : (i + 1) * C]
+        sgu[i, :, 0:C] = gs[i * C : (i + 1) * C].reshape(1, C)
+        sgu[i, :, C:C2] = us[i * C : (i + 1) * C].reshape(1, C)
+    sdn[...] = ds[...].reshape(1, KB)
     igu[...] = 1.0 / (7.0 * sgu[...])
-    idn[...] = 1.0 / (7.0 * ds[...])
+    idn[...] = 1.0 / (7.0 * sdn[...])
     acc[...] = jnp.zeros_like(acc)
     dterm[...] = jnp.zeros_like(dterm)
 
@@ -160,35 +165,27 @@
     for k in (1, 3, 2):
         xcopy(0, k).start()
 
-    def do_quant(i):
+    def quant_rows(w_ref, f_ref, i, keep_ref, keep_at, rows, width, step_of, inv_of):
+        def body(b, carry):
+            at = pl.ds(pl.multiple_of(b * 128, 128), 128)
+            keep = keep_ref[pl.ds(pl.multiple_of(keep_at + b * 128, 128), 128), :] > 0
+            for strip in range(width // 128):
+                lanes = pl.ds(strip * 128, 128)
+                q, f = quant(w_ref[i, at, lanes], step_of(lanes), inv_of(lanes), keep)
+                w_ref[i, at, lanes] = q
+                f_ref[i, at, lanes] = f
+            return carry
+
+        lax.fori_loop(0, rows // 128, body, 0)
+
+    def quant_gate_up(i):
         for cp in weight_copies(i):
             cp.wait()
-        for part in range(2):
-            lanes = pl.ds(part * C, C)
-            step, inv = sgu[i, :, lanes], igu[i, :, lanes]
-
-            def body(b, carry):
-                rows = pl.ds(pl.multiple_of(b * 64, 64), 64)
-                keep = kin[rows, :][:, :1] > 0
-                q, f = quant(wgu[i, rows, lanes], step, inv, keep)
-                wgu[i, rows, lanes] = q
-                fgu[i, rows, lanes] = f
-                return carry
-
-            lax.fori_loop(0, KB // 64, body, 0, unroll=2)
-        for part in range(2):
-            lanes = pl.ds(part * 512, 512)
-            step, inv = ds[:, lanes], idn[:, lanes]
-
-            def body(b, carry):
-                rows = pl.ds(pl.multiple_of(b * 64, 64), 64)
-                keep = khid[pl.ds(pl.multiple_of(i * C + b * 64, 64), 64), :][:, :1] > 0
-                q, f = quant(wd[i, rows, lanes], step, inv, keep)
-                wd[i, rows, lanes] = q
-                fd[i, rows, lanes] = f
-                return carry
-
-            lax.fori_loop(0, C // 64, body, 0, unroll=2)
+        quant_rows(wgu, fgu, i, kin, 0, KB, C2, lambda l: sgu[i, :, l], lambda l: igu[i, :, l])
+
+    def quant_down(i):
+        down_copy(i).wait()
+        quant_rows(wd, fd, i, khid, i * C, C, KB, lambda l: sdn[:, l], lambda l: idn[:, l])
 
     def sib1(i):
         return remote(send1.at[i], recv1.at[i], s1s.at[i], s1r.at[i], sibling)
@@ -210,9 +207,14 @@
 
     def do_pair_sum(i):
         sib1(i).wait_recv()
-        total = pre[i] + recv1[i].astype(F32)
-        pre[i] = total
-        send2[i] = total.astype(BF)
+
+        @pl.loop(0, HALF // BLK)
+        def _(b):
+            rows = pl.ds(pl.multiple_of(b * BLK, BLK), BLK)
+            total = pre[i, rows, :] + recv1[i, rows, :].astype(F32)
+            pre[i, rows, :] = total
+            send2[i, rows, :] = total.astype(BF)
+
         for k in (2, 1, 3):
             ycopy(i, k).start()
 
@@ -255,11 +257,13 @@
             agarrive(i, k).wait_recv()
         sib2(i).start()
 
-    def do_back(i):
+    def do_d_tokens(i):
         sib2(i).wait_recv()
         for n in range(4):
             cols = slice(n * 256, (n + 1) * 256)
             acc[:, cols] += dot_t(act[i, :, 0:C2], wgu[i, cols, :])
+
+    def do_terms(i):
         for n in range(3):
             cols = slice(n * 256, (n + 1) * 256)
             z = dot(tg[0], fgu[i, :, cols])
@@ -270,54 +274,97 @@
             z = dot(act[i, :, C2:C3], fd[i, :, cols])
             dterm[:, cols] += jnp.sum(tg[1, :, cols].astype(F32) * z, axis=0, keepdims=True)
 
-    @pl.loop(0, N + 3)
+    def ecopy(part, k):
+        hi = 1 - zh if part == 0 else zh
+        return remote(
+            esend.at[rows_of(hi * 4 + (x + k) % 4)], erecv.at[part, k - 1],
+            es.at[part, k - 1], er.at[part, k - 1], at_x(x + k, zh),
+        )
+
+    ezcopy = remote(ezsend, ezrecv, ezs, ezr, at_x(x, 1 - zh))
+
+    def start_d_tokens():
+        for part in range(2):
+            for k in (2, 1, 3):
+                rows = rows_of((1 - zh if part == 0 else zh) * 4 + (x + k) % 4)
+                esend[rows, :] = acc[rows, :].astype(BF)
+                ecopy(part, k).start()
+
+    @pl.loop(0, N)
     def _(i):
-        @pl.when(i < N)
-        def _():
-            do_quant(i)
-
-        @pl.when(i == 0)
+        quant_gate_up(i)
+
+        @pl.when(i == 1)
         def _():
             zcopy.wait_recv()
             for k in (1, 3, 2):
                 xcopy(1, k).start()
 
+        @pl.when(i == 3)
+        def _():
+            do_pair_sum(2)
+
         @pl.when(i >= 3)
         def _():
-            do_share(i - 3)
-
-        @pl.when(i == 1)
+            do_act((i - 3) * 2)
+
+        quant_down(i)
+
+        @pl.when(i == 2)
         def _():
             for which in range(2):
                 for k in range(1, 4):
                     xarrive(which, k).wait_recv()
 
-        @pl.when((i >= 1) & (i < N + 1))
-        def _():
-            do_forward(i - 1)
-
-        @pl.when((i >= 2) & (i < N + 2))
-        def _():
-            do_act(i - 2)
-
-        @pl.when((i >= 1) & (i < N + 1))
-        def _():
-            do_pair_sum(i - 1)
+        first = jnp.where(i == 2, 0, i)
+        last = jnp.where(i < 2, i, i + 1)
+
+        @pl.loop(first, last)
+        def _(m):
+            do_forward(m)
+
+            @pl.when((i == 2) & (m >= 1))
+            def _():
+                do_pair_sum(m - 1)
+
+        @pl.when(i == 3)
+        def _():
+            do_act(1)
+
+        @pl.when(i == 4)
+        def _():
+            do_share(0)
 
         @pl.when(i >= 3)
         def _():
-            do_back(i - 3)
-
-    esend[...] = acc[...].astype(BF)
-
-    def ecopy(k):
-        return remote(
-            esend.at[rows_of((dout + k) % 8)], erecv.at[k - 1], es.at[k - 1], er.at[k - 1],
-            (dp, din, (dout + k) % 8),
-        )
-
-    for k in (4, 3, 5, 2, 6, 1, 7):
-        ecopy(k).start()
+            do_pair_sum(i)
+
+    @pl.loop(0, N)
+    def _(i):
+        @pl.when(i == 0)
+        def _():
+            do_share(1)
+            do_act(3)
+
+        @pl.when(i == 2)
+        def _():
+            do_act(4)
+
+        @pl.when(i >= 3)
+        def _():
+            do_share(i)
+
+        do_d_tokens(i)
+
+        @pl.when(i == N - 1)
+        def _():
+            start_d_tokens()
+
+        do_terms(i)
+
+        @pl.when(i == 1)
+        def _():
+            do_share(2)
 
     gslot[din] = gt[...]
     dslot[x] = dterm[...]
@@ -341,6 +388,13 @@
     for k in range(1, 8):
         gcopy(k).start()
     for k in range(1, 4):
+        ecopy(0, k).wait_recv()
+    total = acc[rows_of((dout + 4) % 8), :]
+    for k in range(3):
+        total = total + erecv[0, k].astype(F32)
+    ezsend[...] = total.astype(BF)
+    ezcopy.start()
+    for k in range(1, 4):
         darrive(k).wait_recv()
     part = dslot[0]
     for k in range(1, 4):
@@ -376,21 +430,19 @@
 
     for k in range(1, 4):
         gpcopy(k).start()
-    for k in range(1, 8):
-        ecopy(k).wait_recv()
+    for k in range(1, 4):
+        ecopy(1, k).wait_recv()
     total = acc[rows_of(dout), :]
-    for k in range(7):
-        total = total + erecv[k].astype(F32)
-    dt_out[...] = total.astype(BF)
+    for k in range(3):
+        total = total + erecv[1, k].astype(F32)
+    ezcopy.wait_recv()
+    dt_out[...] = (total + ezrecv[...].astype(F32)).astype(BF)
     for k in range(1, 4):
         gparrive(k).wait_recv()
     part = gdp[0]
     for k in range(1, 4):
         part = part + gdp[k]
-    part = part * SCALE_IN
-    for i in range(N):
-        gg_out[:, i * C : (i + 1) * C] = part[i, :, 0:C]
-        ug_out[:, i * C : (i + 1) * C] = part[i, :, C:C2]
+    gu_out[...] = part * SCALE_IN
     for k in range(1, 8):
         zzarrive(k).wait_recv()
     part = dz[0]
@@ -399,13 +451,14 @@
     dg_out[...] = part * SCALE_HID
 
     zcopy.wait_send()
+    ezcopy.wait_send()
     for k in range(1, 4):
         for which in range(2):
             xcopy(which, k).wait_send()
+            ecopy(which, k).wait_send()
         dcopy(k).wait_send()
         gpcopy(k).wait_send()
     for k in range(1, 8):
-        ecopy(k).wait_send()
         gcopy(k).wait_send()
         zzcopy(k).wait_send()
 
@@ -418,21 +471,28 @@
             agcopy(i, k).wait_send()
 
 
+def place(dt, gu, dg, dt_out, gg_out, ug_out, dg_out):
+    dt_out[...] = dt[...]
+    for i in range(N):
+        gg_out[i * C : (i + 1) * C] = gu[i, :, 0:C].reshape(C)
+        ug_out[i * C : (i + 1) * C] = gu[i, :, C:C2].reshape(C)
+    dg_out[...] = dg[...].reshape(KB)
+
+
 def shards(tokens, out_grad, gate_weight, up_weight, down_weight, gate_step, up_step, down_step, outlier_in, outlier_hidden):
     hbm = pl.BlockSpec(memory_space=pl.ANY)
     vmem = pl.BlockSpec(memory_space=pltpu.VMEM)
     smem = pl.BlockSpec(memory_space=pltpu.SMEM)
     V, S = pltpu.VMEM, pltpu.SemaphoreType.DMA
-    d_tokens, gg, ug, dg = pl.pallas_call(
+    results = pl.pallas_call(
         kernel,
         out_shape=(
             jax.ShapeDtypeStruct((BLK, KB), BF),
-            jax.ShapeDtypeStruct((1, HB), F32),
-            jax.ShapeDtypeStruct((1, HB), F32),
+            jax.ShapeDtypeStruct((N, 1, C2), F32),
             jax.ShapeDtypeStruct((1, KB), F32),
         ),
         in_specs=[hbm, hbm, hbm, hbm, hbm, vmem, vmem, vmem, smem, smem],
-        out_specs=(vmem, vmem, vmem, vmem),
+        out_specs=(vmem, vmem, vmem),
         scratch_shapes=[
             V((2, T, KB), BF),
             V((N, KB, C2), BF),
@@ -444,6 +504,7 @@
             V((N, 1, C2), F32),
             V((N, 1, C2), F32),
             V((1, KB), F32),
+            V((1, KB), F32),
             V((N, HALF, C3), F32),
             V((N, HALF, C3), BF),
             V((N, HALF, C3), BF),
@@ -452,7 +513,9 @@
             V((N, T, C3), BF),
             V((T, KB), F32),
             V((T, KB), BF),
-            V((7, BLK, KB), BF),
+            V((2, 3, BLK, KB), BF),
+            V((BLK, KB), BF),
+            V((BLK, KB), BF),
             V((N, 1, C2), F32),
             V((8, N, 1, C2), F32),
             V((4, N, 1, C2), F32),
@@ -468,7 +531,8 @@
             S((N, 3)), S((N, 3)),
             S((N, 3)), S((N, 3)),
             S((N,)), S((N,)),
-            S((7,)), S((7,)),
+            S((2, 3)), S((2, 3)),
+            S, S,
             S((7,)), S((8,)),
             S((3,)), S((4,)),
             S((3,)), S((4,)),
@@ -480,10 +544,21 @@
         name="swiglu_back",
     )(
         tokens, out_grad, gate_weight, up_weight, down_weight,
-        gate_step.reshape(1, HB), up_step.reshape(1, HB), down_step.reshape(1, KB),
+        gate_step, up_step, down_step,
         outlier_in, outlier_hidden,
     )
-    return d_tokens, gg.reshape(HB), ug.reshape(HB), dg.reshape(KB)
+    return pl.pallas_call(
+        place,
+        out_shape=(
+            jax.ShapeDtypeStruct((BLK, KB), BF),
+            jax.ShapeDtypeStruct((HB,), F32),
+            jax.ShapeDtypeStruct((HB,), F32),
+            jax.ShapeDtypeStruct((KB,), F32),
+        ),
+        in_specs=[vmem] * 3,
+        out_specs=(vmem,) * 4,
+        name="place",
+    )(*results)
 
 
 def solution(mesh):

time: 108 us -> 85.6 us (0.79); the launches traced: 106 us -> 85.4 us
  Pallas kernels: 97.7 us -> 84.7 us
  local copies, waits for them, and re-layouts: 5.34 us -> 0 us
  other arithmetic: 2.63 us -> 0 us
    pallas_call x1, Pallas kernels: 97.7 us -> 83.2 us  [shards(): pl.pallas_call(kernel, out_shape=(jax.ShapeDtypeStruct((BLK, KB), BF), ja...]
    unnamed x2 -> x0, local copies, waits for them, and re-layouts: 2.75 us -> none
    pallas_call x2 -> x0, other arithmetic: 2.63 us -> none  [shards(): pl.pallas_call(kernel, out_shape=(jax.ShapeDtypeStruct((BLK, KB), BF), ja...]
    reshape x2 -> x0, local copies, waits for them, and re-layouts: 2.59 us -> none  [the longest x1 1.3 us: shards(): gate_step.reshape(1, HB)]
    pallas_call x0 -> x1, Pallas kernels: none -> 1.5 us  [shards(): pl.pallas_call(place, out_shape=(jax.ShapeDtypeStruct((BLK, KB), BF), jax...]
where the time goes in v2:
time: 85.6 us; the launch traced here: 85.4 us
  Pallas kernels  84.7 us (99%)
    pallas_call x1, Pallas kernels, shards(): pl.pallas_call(kernel, out_shape=(jax.ShapeDtypeStruct((BLK, KB), BF), ja...  83.2 us

profile of v2, /device:TPU:1, one launch (start us, length us, event | category | flops | bytes accessed | tf_op | source)
XLA Modules:
  0.0 85.4 jit_solution(12879646500578606413)
XLA Ops:
  0.6 83.2 %swiglu_back.1 = (bf16[32,1024]{1,0:T(8,128)(2,1)}, f32[5,1,768]{2,1,0:T(1,128)}, f32[1,1024]{1,0:T(1,128)}) custom-call(bf16[32,1024]{1,0:T(8,128)(2,1)} %tok_hbm.1, bf16[32,1024]{1,0:T(8,128)(2,1)} %og_hbm.1, bf16[1024,1920]{1,0:T(8,128)(2,1)} %gw.1, bf16[1024,1920]{1,0:T(8,128)(2,1)} %uw.1, bf16[1920,1024]{1,0:T(8,128)(2,1)} %dw.1, f32[1920]{0:T(1024)} %gs.1, ...), custom_call_target="tpu_custom_call" | custom-call | tf_op jit(solution)/shard_map/swiglu_back/pallas_call | solution.py:487
  83.9 1.5 %place.1 = (bf16[32,1024]{1,0:T(8,128)(2,1)}, f32[1920]{0:T(1024)}, f32[1920]{0:T(1024)}, f32[1024]{0:T(1024)}) custom-call(bf16[32,1024]{1,0:T(8,128)(2,1)} %get-tuple-element.7.dt, f32[5,1,768]{2,1,0:T(1,128)} %get-tuple-element.8.gu, f32[1,1024]{1,0:T(1,128)} %get-tuple-element.9.dg), custom_call_target="tpu_custom_call" | custom-call | tf_op jit(solution)/shard_map/place/pallas_call | solution.py:550

commit v3 on v2

--- a/solution.py
+++ b/solution.py
@@ -21,6 +21,9 @@
 T = 256
 HALF = T // 2
 BLK = 32
+QTR = 64
+SUB = 16
+SPLIT = 3
 
 MESH = pl.DeviceIdType.MESH
 BF, F32 = jnp.bfloat16, jnp.float32
@@ -86,10 +89,22 @@
 
     sibling = (dp, y * 2 + (1 - c), dout)
 
-    def rows_of(block):
-        return pl.ds(pl.multiple_of((block * BLK + c * HALF) % T, BLK), BLK)
-
-    mine = rows_of(dout)
+    def rows_of(side, k):
+        return pl.ds(pl.multiple_of(side * HALF + ((k % 4) * BLK + c * QTR) % HALF, BLK), BLK)
+
+    barrier = pltpu.get_barrier_semaphore()
+
+    def greet(dev):
+        pl.semaphore_signal(barrier, inc=1, device_id=dev, device_id_type=MESH)
+
+    for k in range(1, 8):
+        greet((dp, (din + k) % 8, dout))
+        greet((dp, din, (dout + k) % 8))
+    for k in range(1, 4):
+        greet(((dp + k) % 4, din, dout))
+        greet(((dp + k) % 4, din, (dout + 4) % 8))
+
+    mine = rows_of(0, x)
     own = [
         pltpu.make_async_copy(tok_hbm, tg.at[0, mine], lsem.at[0]),
         pltpu.make_async_copy(og_hbm, tg.at[1, mine], lsem.at[1]),
@@ -114,58 +129,59 @@
             cp.start()
         down_copy(i).start()
 
-    barrier = pltpu.get_barrier_semaphore()
-
-    def greet(dev):
-        pl.semaphore_signal(barrier, inc=1, device_id=dev, device_id_type=MESH)
-
-    for k in range(1, 8):
-        greet((dp, (din + k) % 8, dout))
-        greet((dp, din, (dout + k) % 8))
-    for k in range(1, 4):
-        greet(((dp + k) % 4, din, dout))
-        greet(((dp + k) % 4, din, (dout + 4) % 8))
-
-    def fill_mask(ref, values, start, rows):
-        @pl.loop(0, rows // 64)
+    def fill_mask(ref, values, start, rows, block):
+        lane = lax.broadcasted_iota(jnp.int32, (block, 128), 1)
+        row = lax.broadcasted_iota(jnp.int32, (block, 128), 0)
+        listed = jnp.full((1, 128), -1, jnp.int32)
+        for k in range(16):
+            listed = jnp.where(lane[:1] == k, values[k] - start, listed)
+        ones = jnp.ones((128, 128), BF)
+
+        @pl.loop(0, rows // block)
         def _(b):
-            idx = lax.broadcasted_iota(jnp.int32, (64, 128), 0) + (b * 64 + start)
-            hit = idx == values[0]
-            for k in range(1, 16):
-                hit = hit | (idx == values[k])
-            ref[pl.ds(pl.multiple_of(b * 64, 64), 64), :] = jnp.where(hit, 1.0, 0.0)
-
-    fill_mask(kin, oi, din * KB, KB)
-    fill_mask(khid, oh, dout * HB, HB)
+            hit = jnp.where(row + b * block == listed, 1.0, 0.0).astype(BF)
+            ref[pl.ds(pl.multiple_of(b * block, block), block), :] = dot(hit, ones)
+
+    fill_mask(kin, oi, din * KB, KB, 256)
+    fill_mask(khid, oh, dout * HB, HB, 384)
+    acc[...] = jnp.zeros_like(acc)
     for i in range(N):
         sgu[i, :, 0:C] = gs[i * C : (i + 1) * C].reshape(1, C)
         sgu[i, :, C:C2] = us[i * C : (i + 1) * C].reshape(1, C)
     sdn[...] = ds[...].reshape(1, KB)
     igu[...] = 1.0 / (7.0 * sgu[...])
     idn[...] = 1.0 / (7.0 * sdn[...])
-    acc[...] = jnp.zeros_like(acc)
     dterm[...] = jnp.zeros_like(dterm)
 
-    pl.semaphore_wait(barrier, 20)
-    for cp in own:
-        cp.wait()
-
-    zcopy = remote(tg.at[:, mine], tg.at[:, mine], zs, zr, at_x(x, 1 - zh))
-    zcopy.start()
-    theirs = rows_of((dout + 4) % 8)
+    theirs = rows_of(1, x)
+    zcopy = remote(tg.at[:, mine], tg.at[:, theirs], zs, zr, at_x(x, 1 - zh))
 
     def xcopy(which, k):
         rows = mine if which == 0 else theirs
         return remote(tg.at[:, rows], tg.at[:, rows], xs.at[which, k - 1], xr.at[which, k - 1], at_x(x + k, zh))
 
     def xarrive(which, k):
-        rows = rows_of((x + 4 - k) % 4 + 4 * (zh if which == 0 else 1 - zh))
+        rows = rows_of(which, x + 4 - k)
         return remote(tg.at[:, rows], tg.at[:, rows], xs.at[which, k - 1], xr.at[which, k - 1], at_x(x + k, zh))
 
-    for k in (1, 3, 2):
-        xcopy(0, k).start()
-
-    def quant_rows(w_ref, f_ref, i, keep_ref, keep_at, rows, width, step_of, inv_of):
+    def start_gather():
+        pl.semaphore_wait(barrier, 20)
+        for cp in own:
+            cp.wait()
+        zcopy.start()
+        for k in (1, 3, 2):
+            xcopy(0, k).start()
+
+    def pass_gather():
+        zcopy.wait_recv()
+        for k in (1, 3, 2):
+            xcopy(1, k).start()
+
+    def wait_gather(which):
+        for k in (1, 3, 2):
+            xarrive(which, k).wait_recv()
+
+    def quant_rows(w_ref, f_ref, i, keep_ref, keep_at, lo, hi, width, step_of, inv_of):
         def body(b, carry):
             at = pl.ds(pl.multiple_of(b * 128, 128), 128)
             keep = keep_ref[pl.ds(pl.multiple_of(keep_at + b * 128, 128), 128), :] > 0
@@ -176,195 +192,239 @@
                 f_ref[i, at, lanes] = f
             return carry
 
-        lax.fori_loop(0, rows // 128, body, 0)
-
-    def quant_gate_up(i):
-        for cp in weight_copies(i):
-            cp.wait()
-        quant_rows(wgu, fgu, i, kin, 0, KB, C2, lambda l: sgu[i, :, l], lambda l: igu[i, :, l])
+        lax.fori_loop(lo // 128, hi // 128, body, 0)
+
+    def quant_gate_up(i, lo, hi):
+        if lo == 0:
+            for cp in weight_copies(i):
+                cp.wait()
+        quant_rows(wgu, fgu, i, kin, 0, lo, hi, C2, lambda l: sgu[i, :, l], lambda l: igu[i, :, l])
 
     def quant_down(i):
         down_copy(i).wait()
-        quant_rows(wd, fd, i, khid, i * C, C, KB, lambda l: sdn[:, l], lambda l: idn[:, l])
-
-    def sib1(i):
-        return remote(send1.at[i], recv1.at[i], s1s.at[i], s1r.at[i], sibling)
-
-    def do_forward(i):
-        for n in range(3):
-            cols = slice(n * 256, (n + 1) * 256)
-            z = dot(tg[0], wgu[i, :, cols])
-            pre[i, :, cols] = z[:HALF]
-            send1[i, :, cols] = z[HALF:].astype(BF)
-        z = dot_t(tg[1], wd[i])
-        pre[i, :, C2:] = z[:HALF]
-        send1[i, :, C2:] = z[HALF:].astype(BF)
-        sib1(i).start()
-
-    def ycopy(i, k):
-        rows = pl.ds(pl.multiple_of(((y + k) % 4) * BLK, BLK), BLK)
-        return remote(send2.at[i, rows], recv2.at[i, k - 1], y2s.at[i, k - 1], y2r.at[i, k - 1], at_y(y + k, c))
-
-    def do_pair_sum(i):
-        sib1(i).wait_recv()
-
-        @pl.loop(0, HALF // BLK)
+        quant_rows(wd, fd, i, khid, i * C, 0, C, KB, lambda l: sdn[:, l], lambda l: idn[:, l])
+
+    def sib1(i, u, n):
+        sides = pl.ds(u, n)
+        return remote(send1.at[i, sides], recv1.at[i, sides], s1s.at[i, u], s1r.at[i, u], sibling)
+
+    def do_forward(i, u, n):
+        def put(z, cols):
+            for v in range(n):
+                pre[i, u + v, :, cols] = z[v * HALF : v * HALF + QTR]
+                send1[i, u + v, :, cols] = z[v * HALF + QTR : (v + 1) * HALF].astype(BF)
+
+        tokens = slice(u * HALF, (u + n) * HALF)
+        for k in range(3):
+            cols = slice(k * 256, (k + 1) * 256)
+            put(dot(tg[0, tokens], wgu[i, :, cols]), cols)
+        put(dot_t(tg[1, tokens], wd[i]), slice(C2, C3))
+        sib1(i, u, n).start()
+
+    def ycopy(i, u, n, k):
+        sides = pl.ds(u, n)
+        rows = pl.ds(pl.multiple_of(((y + k) % 4) * SUB, SUB), SUB)
+        return remote(
+            send2.at[i, sides, rows], recv2.at[i, k - 1, sides],
+            y2s.at[i, u, k - 1], y2r.at[i, u, k - 1], at_y(y + k, c),
+        )
+
+    def do_pair_sum(i, u, n):
+        sib1(i, u, n).wait_recv()
+
+        @pl.loop(0, n * QTR // SUB)
         def _(b):
-            rows = pl.ds(pl.multiple_of(b * BLK, BLK), BLK)
-            total = pre[i, rows, :] + recv1[i, rows, :].astype(F32)
-            pre[i, rows, :] = total
-            send2[i, rows, :] = total.astype(BF)
+            v = u + b // (QTR // SUB)
+            rows = pl.ds(pl.multiple_of((b % (QTR // SUB)) * SUB, SUB), SUB)
+            total = pre[i, v, rows, :] + recv1[i, v, rows, :].astype(F32)
+            pre[i, v, rows, :] = total
+            send2[i, v, rows, :] = total.astype(BF)
 
         for k in (2, 1, 3):
-            ycopy(i, k).start()
-
-    myrow = pl.ds(pl.multiple_of(y * BLK, BLK), BLK)
-
-    def agcopy(i, k):
-        return remote(act.at[i, myrow], act.at[i, myrow], ags.at[i, k - 1], agr.at[i, k - 1], at_y(y + k, c))
-
-    def agarrive(i, k):
-        rows = pl.ds(pl.multiple_of(((y + 4 - k) % 4) * BLK, BLK), BLK)
-        return remote(act.at[i, rows], act.at[i, rows], ags.at[i, k - 1], agr.at[i, k - 1], at_y(y + k, c))
-
-    def do_act(i):
+            ycopy(i, u, n, k).start()
+
+    myrow = pl.ds(pl.multiple_of(y * SUB, SUB), SUB)
+
+    def agcopy(i, u, n, k):
+        ref = act.at[i, pl.ds(u, n), myrow]
+        return remote(ref, ref, ags.at[i, u, k - 1], agr.at[i, u, k - 1], at_y(y + k, c))
+
+    def agarrive(i, u, n, k):
+        rows = pl.ds(pl.multiple_of(((y + 4 - k) % 4) * SUB, SUB), SUB)
+        ref = act.at[i, pl.ds(u, n), rows]
+        return remote(ref, ref, ags.at[i, u, k - 1], agr.at[i, u, k - 1], at_y(y + k, c))
+
+    def do_act(i, u, n):
         for k in (1, 3, 2):
-            ycopy(i, k).wait_recv()
-        own_rows = pre[i, myrow]
-
-        def summed(lo, hi):
-            v = own_rows[:, lo:hi]
-            for k in range(3):
-                v = v + recv2[i, k, :, lo:hi].astype(F32)
-            return v
-
-        gate, up, back = summed(0, C), summed(C, C2), summed(C2, C3)
-        p = jax.nn.sigmoid(gate)
-        gp = gate * p
-        act[i, myrow, 0:C] = (back * up * p * (1.0 + gate * (1.0 - p))).astype(BF)
-        act[i, myrow, C:C2] = (back * gp).astype(BF)
-        act[i, myrow, C2:C3] = (gp * up).astype(BF)
+            ycopy(i, u, n, k).wait_recv()
+        for v in range(u, u + n):
+
+            def summed(lo, hi):
+                total = pre[i, v, myrow, lo:hi]
+                for k in range(3):
+                    total = total + recv2[i, k, v, :, lo:hi].astype(F32)
+                return total
+
+            gate, up, back = summed(0, C), summed(C, C2), summed(C2, C3)
+            p = jax.nn.sigmoid(gate)
+            gp = gate * p
+            act[i, v, myrow, 0:C] = (back * up * p * (1.0 + gate * (1.0 - p))).astype(BF)
+            act[i, v, myrow, C:C2] = (back * gp).astype(BF)
+            act[i, v, myrow, C2:C3] = (gp * up).astype(BF)
         for k in (2, 1, 3):
-            agcopy(i, k).start()
-
-    def sib2(i):
+            agcopy(i, u, n, k).start()
+
+    def sib2(i, u, n):
+        sides = pl.ds(u, n)
         return remote(
-            act.at[i, pl.ds(0, HALF)], act.at[i, pl.ds(HALF, HALF)], s2s.at[i], s2r.at[i], sibling
+            act.at[i, sides, pl.ds(0, QTR)], act.at[i, sides, pl.ds(QTR, QTR)],
+            s2s.at[i, u], s2r.at[i, u], sibling,
         )
 
-    def do_share(i):
+    def do_share(i, u, n):
         for k in (1, 3, 2):
-            agarrive(i, k).wait_recv()
-        sib2(i).start()
+            agarrive(i, u, n, k).wait_recv()
+        sib2(i, u, n).start()
+
+    def act_of(i, lo, hi):
+        return act[i, :, :, lo:hi].reshape(T, hi - lo)
 
     def do_d_tokens(i):
-        sib2(i).wait_recv()
+        @pl.when(i < SPLIT)
+        def _():
+            for u in range(2):
+                sib2(i, u, 1).wait_recv()
+
+        @pl.when(i >= SPLIT)
+        def _():
+            sib2(i, 0, 2).wait_recv()
+
         for n in range(4):
             cols = slice(n * 256, (n + 1) * 256)
-            acc[:, cols] += dot_t(act[i, :, 0:C2], wgu[i, cols, :])
+            acc[:, cols] += dot_t(act_of(i, 0, C2), wgu[i, cols, :])
 
     def do_terms(i):
         for n in range(3):
             cols = slice(n * 256, (n + 1) * 256)
             z = dot(tg[0], fgu[i, :, cols])
-            term = jnp.sum(act[i, :, cols].astype(F32) * z, axis=0, keepdims=True)
+            term = jnp.sum(act_of(i, n * 256, (n + 1) * 256).astype(F32) * z, axis=0, keepdims=True)
             gt[i, :, cols] = term
         for n in range(4):
             cols = slice(n * 256, (n + 1) * 256)
-            z = dot(act[i, :, C2:C3], fd[i, :, cols])
+            z = dot(act_of(i, C2, C3), fd[i, :, cols])
             dterm[:, cols] += jnp.sum(tg[1, :, cols].astype(F32) * z, axis=0, keepdims=True)
 
     def ecopy(part, k):
-        hi = 1 - zh if part == 0 else zh
         return remote(
-            esend.at[rows_of(hi * 4 + (x + k) % 4)], erecv.at[part, k - 1],
+            esend.at[rows_of(1 - part, x + k)], erecv.at[part, k - 1],
             es.at[part, k - 1], er.at[part, k - 1], at_x(x + k, zh),
         )
 
     ezcopy = remote(ezsend, ezrecv, ezs, ezr, at_x(x, 1 - zh))
 
-    def start_d_tokens():
-        for part in range(2):
-            for k in (2, 1, 3):
-                rows = rows_of((1 - zh if part == 0 else zh) * 4 + (x + k) % 4)
-                esend[rows, :] = acc[rows, :].astype(BF)
-                ecopy(part, k).start()
-
-    @pl.loop(0, N)
+    def start_d_tokens(part):
+        for k in (2, 1, 3):
+            rows = rows_of(1 - part, x + k)
+            esend[rows, :] = acc[rows, :].astype(BF)
+            ecopy(part, k).start()
+
+    quant_gate_up(0, 0, KB)
+    start_gather()
+    quant_down(0)
+
+    @pl.loop(1, N)
     def _(i):
-        quant_gate_up(i)
+        quant_gate_up(i, 0, KB // 2)
+
+        @pl.when(i == 2)
+        def _():
+            do_pair_sum(0, 0, 1)
+            do_pair_sum(1, 0, 1)
+
+        @pl.when(i == 3)
+        def _():
+            do_act(1, 0, 1)
+            do_pair_sum(2, 0, 1)
+            wait_gather(1)
+            do_forward(0, 1, 1)
+            do_forward(1, 1, 1)
+
+        @pl.when(i == 4)
+        def _():
+            do_pair_sum(3, 0, 2)
+            do_act(0, 1, 1)
+            do_share(0, 0, 1)
+
+        quant_gate_up(i, KB // 2, KB)
+
+        @pl.when(i == 3)
+        def _():
+            do_pair_sum(0, 1, 1)
+            do_pair_sum(1, 1, 1)
+            do_forward(2, 1, 1)
+
+        @pl.when(i == 4)
+        def _():
+            do_act(1, 1, 1)
+            do_share(1, 0, 1)
+
+        quant_down(i)
 
         @pl.when(i == 1)
         def _():
-            zcopy.wait_recv()
-            for k in (1, 3, 2):
-                xcopy(1, k).start()
+            wait_gather(0)
+            do_forward(0, 0, 1)
+            do_forward(1, 0, 1)
+            pass_gather()
+
+        @pl.when(i == 2)
+        def _():
+            do_forward(2, 0, 1)
+            do_act(0, 0, 1)
 
         @pl.when(i == 3)
         def _():
-            do_pair_sum(2)
+            do_pair_sum(2, 1, 1)
+            do_act(2, 0, 1)
 
         @pl.when(i >= 3)
         def _():
-            do_act((i - 3) * 2)
-
-        quant_down(i)
-
-        @pl.when(i == 2)
-        def _():
-            for which in range(2):
-                for k in range(1, 4):
-                    xarrive(which, k).wait_recv()
-
-        first = jnp.where(i == 2, 0, i)
-        last = jnp.where(i < 2, i, i + 1)
-
-        @pl.loop(first, last)
-        def _(m):
-            do_forward(m)
-
-            @pl.when((i == 2) & (m >= 1))
-            def _():
-                do_pair_sum(m - 1)
-
-        @pl.when(i == 3)
-        def _():
-            do_act(1)
+            do_forward(i, 0, 2)
 
         @pl.when(i == 4)
         def _():
-            do_share(0)
-
-        @pl.when(i >= 3)
-        def _():
-            do_pair_sum(i)
+            do_act(2, 1, 1)
+            do_share(2, 0, 1)
+            do_share(0, 1, 1)
+            do_pair_sum(4, 0, 2)
 
     @pl.loop(0, N)
     def _(i):
         @pl.when(i == 0)
         def _():
-            do_share(1)
-            do_act(3)
-
-        @pl.when(i == 2)
-        def _():
-            do_act(4)
-
-        @pl.when(i >= 3)
-        def _():
-            do_share(i)
+            do_share(1, 1, 1)
+
+        @pl.when(i == 1)
+        def _():
+            do_act(3, 0, 2)
+            do_share(2, 1, 1)
+
+        @pl.when(i == 3)
+        def _():
+            do_act(4, 0, 2)
+            do_share(3, 0, 2)
+
+        @pl.when(i == 4)
+        def _():
+            do_share(4, 0, 2)
 
         do_d_tokens(i)
 
         @pl.when(i == N - 1)
         def _():
-            start_d_tokens()
+            start_d_tokens(0)
 
         do_terms(i)
-
-        @pl.when(i == 1)
-        def _():
-            do_share(2)
 
     gslot[din] = gt[...]
     dslot[x] = dterm[...]
@@ -387,9 +447,10 @@
         dcopy(k).start()
     for k in range(1, 8):
         gcopy(k).start()
+    start_d_tokens(1)
     for k in range(1, 4):
         ecopy(0, k).wait_recv()
-    total = acc[rows_of((dout + 4) % 8), :]
+    total = acc[theirs, :]
     for k in range(3):
         total = total + erecv[0, k].astype(F32)
     ezsend[...] = total.astype(BF)
@@ -432,7 +493,7 @@
         gpcopy(k).start()
     for k in range(1, 4):
         ecopy(1, k).wait_recv()
-    total = acc[rows_of(dout), :]
+    total = acc[mine, :]
     for k in range(3):
         total = total + erecv[1, k].astype(F32)
     ezcopy.wait_recv()
@@ -462,13 +523,13 @@
         gcopy(k).wait_send()
         zzcopy(k).wait_send()
 
-    @pl.loop(0, N)
-    def _(i):
-        sib1(i).wait_send()
-        sib2(i).wait_send()
-        for k in range(1, 4):
-            ycopy(i, k).wait_send()
-            agcopy(i, k).wait_send()
+    for i in range(N):
+        for u, n in ((0, 1), (1, 1)) if i < SPLIT else ((0, 2),):
+            sib1(i, u, n).wait_send()
+            sib2(i, u, n).wait_send()
+            for k in range(1, 4):
+                ycopy(i, u, n, k).wait_send()
+                agcopy(i, u, n, k).wait_send()
 
 
 def place(dt, gu, dg, dt_out, gg_out, ug_out, dg_out):
@@ -505,12 +566,12 @@
             V((N, 1, C2), F32),
             V((1, KB), F32),
             V((1, KB), F32),
-            V((N, HALF, C3), F32),
-            V((N, HALF, C3), BF),
-            V((N, HALF, C3), BF),
-            V((N, HALF, C3), BF),
-            V((N, 3, BLK, C3), BF),
-            V((N, T, C3), BF),
+            V((N, 2, QTR, C3), F32),
+            V((N, 2, QTR, C3), BF),
+            V((N, 2, QTR, C3), BF),
+            V((N, 2, QTR, C3), BF),
+            V((N, 3, 2, SUB, C3), BF),
+            V((N, 2, HALF, C3), BF),
             V((T, KB), F32),
             V((T, KB), BF),
             V((2, 3, BLK, KB), BF),
@@ -527,10 +588,10 @@
             S((N,)),
             S, S,
             S((2, 3)), S((2, 3)),
-            S((N,)), S((N,)),
-            S((N, 3)), S((N, 3)),
-            S((N, 3)), S((N, 3)),
-            S((N,)), S((N,)),
+            S((N, 2)), S((N, 2)),
+            S((N, 2, 3)), S((N, 2, 3)),
+            S((N, 2, 3)), S((N, 2, 3)),
+            S((N, 2)), S((N, 2)),
             S((2, 3)), S((2, 3)),
             S, S,
             S((7,)), S((8,)),

time: 85.6 us -> 79.3 us (0.926)
  Pallas kernels: 84.7 us -> 78.2 us
    pallas_call x1, Pallas kernels: 83.2 us -> 76.7 us  [shards(): pl.pallas_call(kernel, out_shape=(jax.ShapeDtypeStruct((BLK, KB), BF), ja...]
where the time goes in v3:
time: 79.3 us; the launch traced here: 78.8 us
  Pallas kernels  78.2 us (99%)
    pallas_call x1, Pallas kernels, shards(): pl.pallas_call(kernel, out_shape=(jax.ShapeDtypeStruct((BLK, KB), BF), ja...  76.7 us

profile of v3, /device:TPU:1, one launch (start us, length us, event | category | flops | bytes accessed | tf_op | source)
XLA Modules:
  0.0 78.8 jit_solution(18274748334055967447)
XLA Ops:
  0.6 76.7 %swiglu_back.1 = (bf16[32,1024]{1,0:T(8,128)(2,1)}, f32[5,1,768]{2,1,0:T(1,128)}, f32[1,1024]{1,0:T(1,128)}) custom-call(bf16[32,1024]{1,0:T(8,128)(2,1)} %tok_hbm.1, bf16[32,1024]{1,0:T(8,128)(2,1)} %og_hbm.1, bf16[1024,1920]{1,0:T(8,128)(2,1)} %gw.1, bf16[1024,1920]{1,0:T(8,128)(2,1)} %uw.1, bf16[1920,1024]{1,0:T(8,128)(2,1)} %dw.1, f32[1920]{0:T(1024)} %gs.1, ...), custom_call_target="tpu_custom_call" | custom-call | tf_op jit(solution)/shard_map/swiglu_back/pallas_call | solution.py:548
  77.3 1.5 %place.1 = (bf16[32,1024]{1,0:T(8,128)(2,1)}, f32[1920]{0:T(1024)}, f32[1920]{0:T(1024)}, f32[1024]{0:T(1024)}) custom-call(bf16[32,1024]{1,0:T(8,128)(2,1)} %get-tuple-element.7.dt, f32[5,1,768]{2,1,0:T(1,128)} %get-tuple-element.8.gu, f32[1,1024]{1,0:T(1,128)} %get-tuple-element.9.dg), custom_call_target="tpu_custom_call" | custom-call | tf_op jit(solution)/shard_map/place/pallas_call | solution.py:611

commit v4 on v3

--- a/solution.py
+++ b/solution.py
@@ -28,7 +28,8 @@
 MESH = pl.DeviceIdType.MESH
 BF, F32 = jnp.bfloat16, jnp.float32
 
-SIN = (3.14158202, -5.16714276, 2.5418987, -0.55463534)
+K = 0.9 / math.pi
+SIN = tuple(math.sqrt(K) * v for v in (3.14158202, -5.16714276, 2.5418987, -0.55463534))
 
 
 def quant(w, step, inv7, keep):
@@ -43,10 +44,10 @@
         p = p * u + jnp.float32(SIN[k])
     sn = p * r
     s2 = sn * sn
-    d = jnp.maximum(1.0 - s2, 1e-12)
+    d = jnp.maximum(K - s2, 1e-12)
     cs = d * lax.rsqrt(d)
-    shaped = c - sn * cs * jnp.float32(0.9 / math.pi)
-    slope7 = (0.7 + 12.6 * s2) * (1.0 - t * t)
+    shaped = c - sn * cs
+    slope7 = (0.7 + (12.6 / K) * s2) * (1.0 - t * t)
     q = jnp.where(keep, w, step * shaped)
     f = jnp.where(keep, 0.0, shaped - x * slope7)
     return q.astype(BF), f.astype(BF)
@@ -181,28 +182,33 @@
         for k in (1, 3, 2):
             xarrive(which, k).wait_recv()
 
-    def quant_rows(w_ref, f_ref, i, keep_ref, keep_at, lo, hi, width, step_of, inv_of):
+    BOTH, FIRST, SECOND = 0, 1, 2
+
+    def quant_rows(w_ref, f_ref, i, keep_ref, keep_at, lo, hi, width, step_of, inv_of, part):
         def body(b, carry):
             at = pl.ds(pl.multiple_of(b * 128, 128), 128)
             keep = keep_ref[pl.ds(pl.multiple_of(keep_at + b * 128, 128), 128), :] > 0
             for strip in range(width // 128):
                 lanes = pl.ds(strip * 128, 128)
-                q, f = quant(w_ref[i, at, lanes], step_of(lanes), inv_of(lanes), keep)
-                w_ref[i, at, lanes] = q
-                f_ref[i, at, lanes] = f
+                w = (f_ref if part == SECOND else w_ref)[i, at, lanes]
+                q, f = quant(w, step_of(lanes), inv_of(lanes), keep)
+                if part != SECOND:
+                    w_ref[i, at, lanes] = q
+                f_ref[i, at, lanes] = w if part == FIRST else f
             return carry
 
         lax.fori_loop(lo // 128, hi // 128, body, 0)
 
-    def quant_gate_up(i, lo, hi):
-        if lo == 0:
+    def quant_gate_up(i, lo, hi, part=BOTH):
+        if lo == 0 and part != SECOND:
             for cp in weight_copies(i):
                 cp.wait()
-        quant_rows(wgu, fgu, i, kin, 0, lo, hi, C2, lambda l: sgu[i, :, l], lambda l: igu[i, :, l])
-
-    def quant_down(i):
-        down_copy(i).wait()
-        quant_rows(wd, fd, i, khid, i * C, 0, C, KB, lambda l: sdn[:, l], lambda l: idn[:, l])
+        quant_rows(wgu, fgu, i, kin, 0, lo, hi, C2, lambda l: sgu[i, :, l], lambda l: igu[i, :, l], part)
+
+    def quant_down(i, part=BOTH):
+        if part != SECOND:
+            down_copy(i).wait()
+        quant_rows(wd, fd, i, khid, i * C, 0, C, KB, lambda l: sdn[:, l], lambda l: idn[:, l], part)
 
     def sib1(i, u, n):
         sides = pl.ds(u, n)
@@ -289,7 +295,7 @@
     def act_of(i, lo, hi):
         return act[i, :, :, lo:hi].reshape(T, hi - lo)
 
-    def do_d_tokens(i):
+    def wait_share(i):
         @pl.when(i < SPLIT)
         def _():
             for u in range(2):
@@ -299,6 +305,7 @@
         def _():
             sib2(i, 0, 2).wait_recv()
 
+    def do_d_tokens(i):
         for n in range(4):
             cols = slice(n * 256, (n + 1) * 256)
             acc[:, cols] += dot_t(act_of(i, 0, C2), wgu[i, cols, :])
@@ -332,7 +339,7 @@
     start_gather()
     quant_down(0)
 
-    @pl.loop(1, N)
+    @pl.loop(1, N - 1)
     def _(i):
         quant_gate_up(i, 0, KB // 2)
 
@@ -349,12 +356,6 @@
             do_forward(0, 1, 1)
             do_forward(1, 1, 1)
 
-        @pl.when(i == 4)
-        def _():
-            do_pair_sum(3, 0, 2)
-            do_act(0, 1, 1)
-            do_share(0, 0, 1)
-
         quant_gate_up(i, KB // 2, KB)
 
         @pl.when(i == 3)
@@ -362,11 +363,6 @@
             do_pair_sum(0, 1, 1)
             do_pair_sum(1, 1, 1)
             do_forward(2, 1, 1)
-
-        @pl.when(i == 4)
-        def _():
-            do_act(1, 1, 1)
-            do_share(1, 0, 1)
 
         quant_down(i)
 
@@ -386,45 +382,51 @@
         def _():
             do_pair_sum(2, 1, 1)
             do_act(2, 0, 1)
-
-        @pl.when(i >= 3)
-        def _():
-            do_forward(i, 0, 2)
-
-        @pl.when(i == 4)
-        def _():
-            do_act(2, 1, 1)
-            do_share(2, 0, 1)
-            do_share(0, 1, 1)
-            do_pair_sum(4, 0, 2)
-
-    @pl.loop(0, N)
+            do_forward(3, 0, 2)
+
+    last = N - 1
+    quant_gate_up(last, 0, KB // 2, FIRST)
+    do_pair_sum(3, 0, 2)
+    do_act(0, 1, 1)
+    do_share(0, 0, 1)
+    quant_gate_up(last, KB // 2, KB, FIRST)
+    do_act(1, 1, 1)
+    do_share(1, 0, 1)
+    quant_down(last, FIRST)
+    do_forward(last, 0, 2)
+    do_act(2, 1, 1)
+    do_share(2, 0, 1)
+    quant_gate_up(last, 0, KB // 2, SECOND)
+    do_pair_sum(last, 0, 2)
+    do_act(3, 0, 2)
+    quant_gate_up(last, KB // 2, KB, SECOND)
+    do_share(0, 1, 1)
+    do_share(1, 1, 1)
+
+    @pl.loop(0, last)
     def _(i):
-        @pl.when(i == 0)
-        def _():
-            do_share(1, 1, 1)
-
         @pl.when(i == 1)
         def _():
-            do_act(3, 0, 2)
             do_share(2, 1, 1)
 
+        @pl.when(i == 2)
+        def _():
+            do_act(last, 0, 2)
+
         @pl.when(i == 3)
         def _():
-            do_act(4, 0, 2)
+            quant_down(last, SECOND)
             do_share(3, 0, 2)
-
-        @pl.when(i == 4)
-        def _():
-            do_share(4, 0, 2)
-
+            do_share(last, 0, 2)
+
+        wait_share(i)
         do_d_tokens(i)
-
-        @pl.when(i == N - 1)
-        def _():
-            start_d_tokens(0)
-
         do_terms(i)
+
+    wait_share(last)
+    do_d_tokens(last)
+    start_d_tokens(0)
+    do_terms(last)
 
     gslot[din] = gt[...]
     dslot[x] = dterm[...]
@@ -448,6 +450,42 @@
     for k in range(1, 8):
         gcopy(k).start()
     start_d_tokens(1)
+    for k in range(1, 8):
+        garrive(k).wait_recv()
+    part = gslot[0]
+    for k in range(1, 8):
+        part = part + gslot[k]
+    gdp[dp] = part
+
+    def gpcopy(k):
+        return remote(gdp.at[dp], gdp.at[dp], gp_s.at[k - 1], gp_r.at[dp], ((dp + k) % 4, din, dout))
+
+    def gparrive(k):
+        src = (dp + k) % 4
+        return remote(gdp.at[src], gdp.at[src], gp_s.at[k - 1], gp_r.at[src], (src, din, dout))
+
+    for k in range(1, 4):
+        gpcopy(k).start()
+    for k in range(1, 4):
+        darrive(k).wait_recv()
+    part = dslot[0]
+    for k in range(1, 4):
+        part = part + dslot[k]
+    zi = zh * 4 + dp
+    dz[zi] = part
+
+    def at_z(k):
+        return (k % 4, din, (k // 4) * 4 + x)
+
+    def zzcopy(k):
+        return remote(dz.at[zi], dz.at[zi], dz_s.at[k - 1], dz_r.at[zi], at_z((zi + k) % 8))
+
+    def zzarrive(k):
+        src = (zi + k) % 8
+        return remote(dz.at[src], dz.at[src], dz_s.at[k - 1], dz_r.at[src], at_z(src))
+
+    for k in range(1, 8):
+        zzcopy(k).start()
     for k in range(1, 4):
         ecopy(0, k).wait_recv()
     total = acc[theirs, :]
@@ -455,42 +493,6 @@
         total = total + erecv[0, k].astype(F32)
     ezsend[...] = total.astype(BF)
     ezcopy.start()
-    for k in range(1, 4):
-        darrive(k).wait_recv()
-    part = dslot[0]
-    for k in range(1, 4):
-        part = part + dslot[k]
-    zi = zh * 4 + dp
-    dz[zi] = part
-
-    def at_z(k):
-        return (k % 4, din, (k // 4) * 4 + x)
-
-    def zzcopy(k):
-        return remote(dz.at[zi], dz.at[zi], dz_s.at[k - 1], dz_r.at[zi], at_z((zi + k) % 8))
-
-    def zzarrive(k):
-        src = (zi + k) % 8
-        return remote(dz.at[src], dz.at[src], dz_s.at[k - 1], dz_r.at[src], at_z(src))
-
-    for k in range(1, 8):
-        zzcopy(k).start()
-    for k in range(1, 8):
-        garrive(k).wait_recv()
-    part = gslot[0]
-    for k in range(1, 8):
-        part = part + gslot[k]
-    gdp[dp] = part
-
-    def gpcopy(k):
-        return remote(gdp.at[dp], gdp.at[dp], gp_s.at[k - 1], gp_r.at[dp], ((dp + k) % 4, din, dout))
-
-    def gparrive(k):
-        src = (dp + k) % 4
-        return remote(gdp.at[src], gdp.at[src], gp_s.at[k - 1], gp_r.at[src], (src, din, dout))
-
-    for k in range(1, 4):
-        gpcopy(k).start()
     for k in range(1, 4):
         ecopy(1, k).wait_recv()
     total = acc[mine, :]

time: 79.3 us -> 79.3 us (level)
  no operation moved by 1% of the time
where the time goes in v4:
time: 79.3 us; the launch traced here: 78.3 us
  Pallas kernels  77.6 us (98%)
    pallas_call x1, Pallas kernels, shards(): pl.pallas_call(kernel, out_shape=(jax.ShapeDtypeStruct((BLK, KB), BF), ja...  76.1 us

profile of v4, /device:TPU:1, one launch (start us, length us, event | category | flops | bytes accessed | tf_op | source)
XLA Modules:
  0.0 78.3 jit_solution(13080082893434971126)
XLA Ops:
  0.6 76.1 %swiglu_back.1 = (bf16[32,1024]{1,0:T(8,128)(2,1)}, f32[5,1,768]{2,1,0:T(1,128)}, f32[1,1024]{1,0:T(1,128)}) custom-call(bf16[32,1024]{1,0:T(8,128)(2,1)} %tok_hbm.1, bf16[32,1024]{1,0:T(8,128)(2,1)} %og_hbm.1, bf16[1024,1920]{1,0:T(8,128)(2,1)} %gw.1, bf16[1024,1920]{1,0:T(8,128)(2,1)} %uw.1, bf16[1920,1024]{1,0:T(8,128)(2,1)} %dw.1, f32[1920]{0:T(1024)} %gs.1, ...), custom_call_target="tpu_custom_call" | custom-call | tf_op jit(solution)/shard_map/swiglu_back/pallas_call | solution.py:550
  76.8 1.5 %place.1 = (bf16[32,1024]{1,0:T(8,128)(2,1)}, f32[1920]{0:T(1024)}, f32[1920]{0:T(1024)}, f32[1024]{0:T(1024)}) custom-call(bf16[32,1024]{1,0:T(8,128)(2,1)} %get-tuple-element.7.dt, f32[5,1,768]{2,1,0:T(1,128)} %get-tuple-element.8.gu, f32[1,1024]{1,0:T(1,128)} %get-tuple-element.9.dg), custom_call_target="tpu_custom_call" | custom-call | tf_op jit(solution)/shard_map/place/pallas_call | solution.py:613

commit v5 on v4

--- a/solution.py
+++ b/solution.py
@@ -310,12 +310,14 @@
             cols = slice(n * 256, (n + 1) * 256)
             acc[:, cols] += dot_t(act_of(i, 0, C2), wgu[i, cols, :])
 
-    def do_terms(i):
+    def do_gate_terms(i):
         for n in range(3):
             cols = slice(n * 256, (n + 1) * 256)
             z = dot(tg[0], fgu[i, :, cols])
             term = jnp.sum(act_of(i, n * 256, (n + 1) * 256).astype(F32) * z, axis=0, keepdims=True)
             gt[i, :, cols] = term
+
+    def do_down_terms(i):
         for n in range(4):
             cols = slice(n * 256, (n + 1) * 256)
             z = dot(act_of(i, C2, C3), fd[i, :, cols])
@@ -421,14 +423,12 @@
 
         wait_share(i)
         do_d_tokens(i)
-        do_terms(i)
+        do_gate_terms(i)
+        do_down_terms(i)
 
     wait_share(last)
-    do_d_tokens(last)
-    start_d_tokens(0)
-    do_terms(last)
-
-    gslot[din] = gt[...]
+    do_down_terms(last)
+
     dslot[x] = dterm[...]
 
     def gcopy(k):
@@ -447,9 +447,33 @@
 
     for k in range(1, 4):
         dcopy(k).start()
+    do_d_tokens(last)
+    start_d_tokens(0)
+    do_gate_terms(last)
+    gslot[din] = gt[...]
     for k in range(1, 8):
         gcopy(k).start()
     start_d_tokens(1)
+    for k in range(1, 4):
+        darrive(k).wait_recv()
+    part = dslot[0]
+    for k in range(1, 4):
+        part = part + dslot[k]
+    zi = zh * 4 + dp
+    dz[zi] = part
+
+    def at_z(k):
+        return (k % 4, din, (k // 4) * 4 + x)
+
+    def zzcopy(k):
+        return remote(dz.at[zi], dz.at[zi], dz_s.at[k - 1], dz_r.at[zi], at_z((zi + k) % 8))
+
+    def zzarrive(k):
+        src = (zi + k) % 8
+        return remote(dz.at[src], dz.at[src], dz_s.at[k - 1], dz_r.at[src], at_z(src))
+
+    for k in range(1, 8):
+        zzcopy(k).start()
     for k in range(1, 8):
         garrive(k).wait_recv()
     part = gslot[0]
@@ -466,26 +490,6 @@
 
     for k in range(1, 4):
         gpcopy(k).start()
-    for k in range(1, 4):
-        darrive(k).wait_recv()
-    part = dslot[0]
-    for k in range(1, 4):
-        part = part + dslot[k]
-    zi = zh * 4 + dp
-    dz[zi] = part
-
-    def at_z(k):
-        return (k % 4, din, (k // 4) * 4 + x)
-
-    def zzcopy(k):
-        return remote(dz.at[zi], dz.at[zi], dz_s.at[k - 1], dz_r.at[zi], at_z((zi + k) % 8))
-
-    def zzarrive(k):
-        src = (zi + k) % 8
-        return remote(dz.at[src], dz.at[src], dz_s.at[k - 1], dz_r.at[src], at_z(src))
-
-    for k in range(1, 8):
-        zzcopy(k).start()
     for k in range(1, 4):
         ecopy(0, k).wait_recv()
     total = acc[theirs, :]

time: 79.3 us -> 79.2 us (level)
  no operation moved by 1% of the time
where the time goes in v5:
time: 79.2 us; the launch traced here: 78.5 us
  Pallas kernels  77.8 us (98%)
    pallas_call x1, Pallas kernels, shards(): pl.pallas_call(kernel, out_shape=(jax.ShapeDtypeStruct((BLK, KB), BF), ja...  76.3 us

profile of v5, /device:TPU:1, one launch (start us, length us, event | category | flops | bytes accessed | tf_op | source)
XLA Modules:
  0.0 78.5 jit_solution(17890109333498464818)
XLA Ops:
  0.6 76.3 %swiglu_back.1 = (bf16[32,1024]{1,0:T(8,128)(2,1)}, f32[5,1,768]{2,1,0:T(1,128)}, f32[1,1024]{1,0:T(1,128)}) custom-call(bf16[32,1024]{1,0:T(8,128)(2,1)} %tok_hbm.1, bf16[32,1024]{1,0:T(8,128)(2,1)} %og_hbm.1, bf16[1024,1920]{1,0:T(8,128)(2,1)} %gw.1, bf16[1024,1920]{1,0:T(8,128)(2,1)} %uw.1, bf16[1920,1024]{1,0:T(8,128)(2,1)} %dw.1, f32[1920]{0:T(1024)} %gs.1, ...), custom_call_target="tpu_custom_call" | custom-call | tf_op jit(solution)/shard_map/swiglu_back/pallas_call | solution.py:554
  77.0 1.5 %place.1 = (bf16[32,1024]{1,0:T(8,128)(2,1)}, f32[1920]{0:T(1024)}, f32[1920]{0:T(1024)}, f32[1024]{0:T(1024)}) custom-call(bf16[32,1024]{1,0:T(8,128)(2,1)} %get-tuple-element.7.dt, f32[5,1,768]{2,1,0:T(1,128)} %get-tuple-element.8.gu, f32[1,1024]{1,0:T(1,128)} %get-tuple-element.9.dg), custom_call_target="tpu_custom_call" | custom-call | tf_op jit(solution)/shard_map/place/pallas_call | solution.py:617
